TPU v7x, 512 devices: a whole 4x4x16 slice. The times are simulated.
512 devices in a mesh: ctx: 128 (over z, x, y_lo), doc: 4 (over y_hi, core).
Axes of the slice: x: 4, y: 4 (y_hi: 2, y_lo: 2; y = y_hi * 2 + y_lo), z: 16, core: 2. Of those that a mesh axis runs over, the one named last changes fastest.
Arguments:
- teacher_hidden: bfloat16 [131072, 5120], P(('doc', 'ctx')), parts along dimension 0, may hold values from -6 to 6
- teacher_gain: float32 [5120], replicated, may hold values from 0.5 to 2
- group_proj: bfloat16 [5120, 512], P('ctx'), may hold values from -0.25 to 0.25
- student_hidden: bfloat16 [65536, 4096], P(('doc', 'ctx')), parts along dimension 0, may hold values from -6 to 6
- student_gain: float32 [4096], replicated, may hold values from 0.5 to 2
- student_count: int32 [512], P(('doc', 'ctx')), parts along dimension 0, may hold values from 64 to 128, as said below
- spans: int32 [65536, 8], P(('doc', 'ctx')), parts along dimension 0, may hold values from -1 to 32767, as said below
- span_len: int32 [65536], P(('doc', 'ctx')), parts along dimension 0, may hold values from 0 to 8, as said below
Outputs:
- grad_rows: bfloat16 [65536, 4096], P(('doc', 'ctx')), parts along dimension 0
- grad_gain: float32 [16384], P(('doc', 'ctx')), parts along dimension 0
- loss: float32 [4], P('doc'), parts along dimension 0
There are 4 independent parts, one for each index of `doc`. A program takes and returns all parts, laid end to end along the dimension named above; an argument that names none is the same for every part. Nothing has to cross between parts.
Inputs may be any that keep to these rules, and one draw needn't show every extreme that they name: Slots 0 to student_count - 1 of a device's 128 slots hold tokens, the others are padding. `span_len`: 0 exactly on padding slots. `spans`: for a live slot on device i, entries 0 to span_len - 1 are consecutive rising teacher indices within i * 256 - 64 to (i + 1) * 256 + 63, clipped to the document; every other entry is -1.
All inputs are finite; a program needn't handle non-finite values.
Results may differ from a plain program's by a relative error of at most 0.0048.
Values may be sent and summed in bfloat16 or wider, within the bound.
No kernel may reach another device: no remote copies, remote signals or barrier semaphores. Data moves between devices by JAX's collectives and lax.ppermute only.
A program may use at most 64 MiB of HBM per device.

v0:
```python
import jax
import jax.numpy as jnp
from jax import lax
from jax.sharding import PartitionSpec as P

HD = 128
SH = 32
KVG = 8
SPAN = 8
TG = 5
SG = 4
HALO = 64


def with_halo(cells, sides, width):
    for axis, dim in sides:
        count = lax.axis_size(axis)
        ends = count - 1
        head = lax.slice_in_dim(cells, 0, width, axis=dim)
        tail = lax.slice_in_dim(cells, cells.shape[dim] - width, cells.shape[dim], axis=dim)
        cells = jnp.concatenate(
            [
                lax.ppermute(tail, axis, [(i, (i + 1) % count) for i in range(ends)]),
                cells,
                lax.ppermute(head, axis, [((i + 1) % count, i) for i in range(ends)]),
            ],
            axis=dim,
        )
    return cells


def normalize(teacher_hidden, teacher_gain):
    teacher_float = teacher_hidden.astype(jnp.float32)
    teacher_scale = lax.rsqrt(
        jnp.mean(teacher_float * teacher_float, axis=-1, keepdims=True) + 1e-05
    )
    return (teacher_float * teacher_scale * teacher_gain).astype(jnp.bfloat16)


def project(normed_rows, blocks):
    row_count = normed_rows.shape[0]
    split_rows = normed_rows.reshape(row_count, KVG, TG * HD)
    mixed_rows = jnp.einsum("rgk,gkm->rgm", split_rows, blocks, preferred_element_type=jnp.float32)
    return mixed_rows.reshape(row_count, SH * HD).astype(jnp.bfloat16)


def per_device(
    teacher_hidden,
    teacher_gain,
    group_proj,
    student_hidden,
    student_gain,
    student_count,
    spans,
    span_len,
):
    row_count = teacher_hidden.shape[0]
    teacher_normed = normalize(teacher_hidden, teacher_gain)
    whole_proj = lax.all_gather(group_proj, "ctx", axis=0, tiled=True)
    blocks = whole_proj.reshape(KVG, TG * HD, SG * HD)
    own_rows = project(teacher_normed, blocks)
    gathered = with_halo(teacher_normed, (("ctx", 0),), HALO)
    lower_rows = project(gathered[:HALO], blocks)
    upper_rows = project(gathered[HALO + row_count :], blocks)
    extended = jnp.concatenate([lower_rows, own_rows, upper_rows], axis=0)
    offset_rows = lax.axis_index("ctx") * row_count - HALO
    local_index = jnp.clip(spans - offset_rows, 0, extended.shape[0] - 1)
    pooled = jnp.zeros((spans.shape[0], extended.shape[1]), jnp.float32)
    for column in range(SPAN):
        weight_entry = (span_len > column).astype(jnp.float32)[:, None]
        pooled = pooled + extended[local_index[:, column]].astype(jnp.float32) * weight_entry
    pooled = pooled / jnp.maximum(span_len, 1).astype(jnp.float32)[:, None]
    slot_count = student_hidden.shape[0]
    live_mask = (jnp.arange(slot_count, dtype=jnp.int32) < student_count[0]).astype(jnp.float32)[
        :, None
    ]
    student_float = student_hidden.astype(jnp.float32)
    inv_rms = lax.rsqrt(jnp.mean(student_float * student_float, axis=-1, keepdims=True) + 1e-05)
    normed_student = student_float * inv_rms
    mismatch = live_mask * (normed_student * student_gain - pooled)
    scaled = mismatch * student_gain
    inner_mean = jnp.mean(scaled * normed_student, axis=-1, keepdims=True)
    grad_rows = (inv_rms * (scaled - normed_student * inner_mean)).astype(jnp.bfloat16)
    gain_terms = jnp.sum(mismatch * normed_student, axis=0)
    square_local = jnp.sum(mismatch * mismatch)
    count_local = student_count.astype(jnp.float32)[0]
    square_total, live_total = lax.psum((square_local, count_local), "ctx")
    gain_part = lax.psum_scatter(gain_terms, "ctx", scatter_dimension=0, tiled=True)
    grad_gain = gain_part / live_total
    loss = (square_total / (SH * HD * live_total)).reshape(1)
    return (grad_rows, grad_gain, loss)


def solution(mesh):
    placed = (
        P(("doc", "ctx"), None),
        P(),
        P("ctx", None),
        P(("doc", "ctx"), None),
        P(),
        P(("doc", "ctx")),
        P(("doc", "ctx"), None),
        P(("doc", "ctx")),
    )
    return jax.shard_map(
        per_device,
        mesh=mesh,
        in_specs=placed,
        out_specs=(P(("doc", "ctx"), None), P(("doc", "ctx")), P("doc")),
        check_vma=False,
    )
```

profile of v0, /device:TPU:16, one launch (start us, length us, event | category | flops | bytes accessed | tf_op | source)
XLA Modules:
  0.0 1278.1 jit_solution(5116301238375197107)
XLA Ops:
  7.2 0.0 copy-start.1
  7.2 0.0 copy-start.7
  7.2 0.0 all-gather.2.cloned.1.call-start
  7.2 0.7 all-gather.2.cloned.1.call-update
  7.9 2.4 fusion
  10.3 0.0 copy-done.1
  10.3 0.0 copy-done.7
  10.3 0.8 fusion.2
  11.1 0.0 copy-start.4
  11.1 1.5 copy-done.4
  12.6 0.0 copy-start.8
  12.6 0.0 copy-start.2
  12.6 0.0 copy-start.9
  12.6 0.9 fusion.35
  13.5 3.2 collective-permute-start
  16.7 1.3 collective-permute-start.1
  18.1 0.0 copy-done.8
  18.1 0.0 copy-done.2
  18.1 0.3 fusion.17
  18.4 0.0 copy-done.9
  19.1 1.3 dynamic-slice
  21.1 27.3 %collective-permute-done = bf16[64,5120]{1,0:T(8,128)(2,1)S(1)} collective-permute-done((bf16[64,5120]{1,0:T(8,128)(2,1)}, bf16[64,5120]{1,0:T(8,128)(2,1)S(1)}, u32[]{:S(2)}, u32[]{:S(2)}) %collective-permute-start) | collective-permute-done | bytes 655392 | tf_op jit(solution)/shard_map/ppermute | solution.py:23
  48.4 572.1 %all-gather.2.cloned.1.call-done = bf16[5120,512]{1,0:T(8,128)(2,1)} async-done(((bf16[40,512]{1,0:T(8,128)(2,1)}), bf16[5120,512]{1,0:T(8,128)(2,1)}) %all-gather.2.cloned.1.call-update) | async-done | bytes 5242896 | tf_op jit(solution)/shard_map/all_gather | solution.py:59
  620.5 0.0 copy-start
  620.5 3.7 fusion.20
  624.2 0.9 copy.29
  625.1 0.0 collective-permute-done.1
  625.1 0.0 copy-done
  625.1 0.0 copy-start.5
  625.1 1.0 fusion.21
  626.1 0.8 copy.30
  626.9 0.0 copy-done.5
  626.9 3.2 convert_bitcast_fusion
  630.1 2.8 copy.22
  632.9 3.0 copy.25
  635.9 2.0 pad_maximum_fusion
  637.9 2.2 gather_fusion
  640.1 2.2 gather_fusion.1
  642.3 2.2 gather_fusion.2
  644.4 2.2 gather_fusion.3
  646.6 2.2 gather_fusion.4
  648.8 2.2 gather_fusion.5
  651.0 2.2 gather_fusion.6
  653.2 0.0 copy-start.6
  653.2 2.2 gather_fusion.7
  655.4 0.0 copy-done.6
  655.4 0.0 copy-start.3
  655.4 6.1 fusion.16
  661.5 604.6 %all-reduce.1 = (f32[4096]{0:T(1024)S(1)}, f32[]{:T(128)}, f32[]{:T(128)}) all-reduce(f32[4096]{0:T(1024)S(1)} %get-tuple-element.3, f32[]{:T(128)} %bitcast.14, f32[]{:T(128)} %get-tuple-element.5), channel_id=2, replica_groups=mesh['ctx'=128,'doc'=4] {'ctx'}, use_global_device_ids=true, to_apply=%region_4.5.clone | all-reduce | flops 4098 | bytes 32784
  1267.4 1.2 dynamic-slice_divide_fusion
  1268.6 0.0 copy-done.3
  1268.6 1.5 fusion.15
  (11 shorter events, 0.1 us)
Async XLA Ops:
  7.2 3.2 copy-start.1
  7.2 3.1 copy-start.7
  7.2 613.3 %all-gather.2.cloned.1.call-start = ((), (), s32[]{:S(2)}) async-start(), calls=%async_computation | async-start | bytes 5283840 | tf_op jit(solution)/shard_map/all_gather | solution.py:59
  11.1 1.5 copy-start.4
  12.6 5.5 copy-start.8
  12.6 5.5 copy-start.2
  12.6 5.8 copy-start.9
  13.5 34.9 %collective-permute-start = (bf16[64,5120]{1,0:T(8,128)(2,1)}, bf16[64,5120]{1,0:T(8,128)(2,1)S(1)}, u32[]{:S(2)}, u32[]{:S(2)}) collective-permute-start(bf16[64,5120]{1,0:T(8,128)(2,1)} %get-tuple-element.10), channel_id=1, source_target_pairs={{0,4},{4,8},{8,12},{12,16},{16,20},{20,24},{24,28},{28,32},{32,36}... | collective-permute-start | bytes 1966088 | tf_op jit(solution)/shard_map/ppermute | solution.py:23
  16.7 608.3 %collective-permute-start.1 = (bf16[64,5120]{1,0:T(8,128)(2,1)S(1)}, bf16[64,5120]{1,0:T(8,128)(2,1)S(1)}, u32[]{:S(2)}, u32[]{:S(2)}) collective-permute-start(bf16[64,5120]{1,0:T(8,128)(2,1)S(1)} %get-tuple-element.11), channel_id=1, source_target_pairs={{4,0},{8,4},{12,8},{16,12},{20,16},{24,20},{28,24},{32,28},{36,32}... | collective-permute-start | bytes 1966088 | tf_op jit(solution)/shard_map/ppermute | solution.py:25
  620.5 4.6 copy-start
  625.1 1.9 copy-start.5
  653.2 2.2 copy-start.6
  655.4 613.3 %copy-start.3 = (bf16[128,4096]{1,0:T(8,128)(2,1)S(1)}, bf16[128,4096]{1,0:T(8,128)(2,1)}, u32[]{:S(2)}) copy-start(bf16[128,4096]{1,0:T(8,128)(2,1)} %param.11) | copy-start | bytes 3145732
Sparse Core Ops, SparseCore 0:
  10.1 610.3 all-gather.1
where the time goes:
time: 1280 us
  blocking collectives  605 us (47%)
  waiting for transfers between devices  600 us (47%)
  local copies, waits for them, and re-layouts  28.8 us (2%)
  between operations  17.9 us (1%)
  other arithmetic  14.3 us (1%)
    unnamed x1, blocking collectives  605 us
    all_gather x1, waiting for transfers between devices, per_device(): whole_proj = lax.all_gather(group_proj, 'ctx', axis=0, tiled=True)  572 us
    ppermute x1, waiting for transfers between devices, with_halo(): lax.ppermute(tail, axis, [(i, (i + 1) % count) for i in range(ends)])  27.3 us
  transfers between devices with their start and end apart: 3, of which 2 were waited for; matrix products, arithmetic and copies ran while one was open for 1% of the time, Pallas kernels for 0%

commit v1 on v0

v1 whole, which is shorter than its diff:
```python
import jax
import jax.numpy as jnp
from jax import lax
from jax.sharding import Mesh
from jax.sharding import PartitionSpec as P

HD = 128
SH = 32
KVG = 8
SPAN = 8
TG = 5
SG = 4
HALO = 64
NZ = 16
NX = 4
NY = 2
CTX = ("z", "x", "ylo")
PART = ("yhi", "core")
SWAP = [(0, 1), (1, 0)]


def shared(cells, count):
    return jnp.broadcast_to(cells[None], (count,) + cells.shape)


def gather_columns(group_proj):
    half = SG * HD // 2
    mine = lax.dynamic_slice_in_dim(group_proj, lax.axis_index("core") * half, half, axis=1)
    line = lax.all_to_all(shared(mine, NZ), "z", 0, 0)
    plane = lax.all_to_all(shared(line, NX * NY), ("x", "ylo"), 0, 0)
    return plane.transpose(1, 0, 2, 3).reshape(KVG, TG * HD, half)


def normalize(teacher_hidden, teacher_gain):
    teacher_float = teacher_hidden.astype(jnp.float32)
    teacher_scale = lax.rsqrt(
        jnp.mean(teacher_float * teacher_float, axis=-1, keepdims=True) + 1e-05
    )
    return (teacher_float * teacher_scale * teacher_gain).astype(jnp.bfloat16)


def per_device(
    teacher_hidden,
    teacher_gain,
    group_proj,
    student_hidden,
    student_gain,
    student_count,
    spans,
    span_len,
):
    row_count = teacher_hidden.shape[0]
    slot_count = student_hidden.shape[0]
    half = SG * HD // 2
    core = lax.axis_index("core")
    devices = NZ * NX * NY

    up = [(i, (i + 1) % devices) for i in range(devices)]
    down = [((i + 1) % devices, i) for i in range(devices)]
    lower = lax.ppermute(teacher_hidden[row_count - HALO :], CTX, up)
    upper = lax.ppermute(teacher_hidden[:HALO], CTX, down)

    weights = gather_columns(group_proj)

    offset_rows = lax.axis_index(CTX) * row_count - HALO
    local_index = spans - offset_rows
    live_entry = jnp.arange(SPAN, dtype=jnp.int32)[None, :] < span_len[:, None]
    local_index = jnp.where(live_entry, local_index, -1)

    def counts(first, rows):
        wanted = jnp.arange(rows, dtype=jnp.int32) + first
        hits = local_index[:, :, None] == wanted[None, None, :]
        return jnp.sum(hits.astype(jnp.float32), axis=1).astype(jnp.bfloat16)

    def summed(first, rows):
        return jnp.dot(
            counts(first, rows.shape[0]),
            normalize(rows, teacher_gain),
            preferred_element_type=jnp.float32,
        )

    total = summed(HALO, teacher_hidden)
    total = total + summed(0, lower)
    total = total + summed(HALO + row_count, upper)
    share = 1.0 / jnp.maximum(span_len, 1).astype(jnp.float32)[:, None]
    pooled_normed = (total * share).astype(jnp.bfloat16)

    other_normed = lax.ppermute(pooled_normed, "core", SWAP)
    both = jnp.concatenate([pooled_normed, other_normed], axis=0)
    both = both.reshape(2 * slot_count, KVG, TG * HD)
    mixed = jnp.einsum("rgk,gkm->rgm", both, weights, preferred_element_type=jnp.float32)
    own = mixed[:slot_count].astype(jnp.bfloat16)
    back = lax.ppermute(mixed[slot_count:].astype(jnp.bfloat16), "core", SWAP)
    low = jnp.where(core == 0, own, back)
    high = jnp.where(core == 0, back, own)
    pooled = jnp.concatenate([low, high], axis=2).reshape(slot_count, SH * HD)
    pooled = pooled.astype(jnp.float32)

    live_mask = (jnp.arange(slot_count, dtype=jnp.int32) < student_count[0]).astype(jnp.float32)[
        :, None
    ]
    student_float = student_hidden.astype(jnp.float32)
    inv_rms = lax.rsqrt(jnp.mean(student_float * student_float, axis=-1, keepdims=True) + 1e-05)
    normed_student = student_float * inv_rms
    mismatch = live_mask * (normed_student * student_gain - pooled)
    scaled = mismatch * student_gain
    inner_mean = jnp.mean(scaled * normed_student, axis=-1, keepdims=True)
    grad_rows = (inv_rms * (scaled - normed_student * inner_mean)).astype(jnp.bfloat16)
    gain_terms = jnp.sum(mismatch * normed_student, axis=0)
    square_local = jnp.sum(mismatch * mismatch)
    count_local = student_count.astype(jnp.float32)[0]

    piece = SH * HD // devices
    terms = gain_terms.reshape(NZ, NX * NY, piece).transpose(1, 0, 2)
    tail = jnp.broadcast_to(
        jnp.stack([square_local, count_local])[None, None, :], (NX * NY, NZ, 2)
    )
    terms = jnp.concatenate([terms, tail], axis=2)
    terms = jnp.sum(lax.all_to_all(terms, ("x", "ylo"), 0, 0), axis=0)
    terms = jnp.sum(lax.all_to_all(terms, "z", 0, 0), axis=0)
    live_total = terms[piece + 1]
    grad_gain = terms[:piece] / live_total
    loss = (terms[piece] / (SH * HD * live_total)).reshape(1)
    return (grad_rows, grad_gain, loss)


def solution(mesh):
    fine = Mesh(mesh.devices.reshape(NZ, NX, NY, 2, 2), CTX + PART)
    every = PART + CTX
    placed = (
        P(every, None),
        P(),
        P(CTX, None),
        P(every, None),
        P(),
        P(every),
        P(every, None),
        P(every),
    )
    return jax.shard_map(
        per_device,
        mesh=fine,
        in_specs=placed,
        out_specs=(P(every, None), P(every), P(PART)),
        check_vma=False,
    )
```

time: 1280 us -> 157 us (0.12)
  blocking collectives: 605 us -> 0 us
  waiting for transfers between devices: 600 us -> 69.9 us
  starting transfers between devices: 4.54 us -> 47.9 us
  local copies, waits for them, and re-layouts: 28.8 us -> 12.6 us
  between operations: 17.9 us -> 4.08 us
    unnamed x1 -> x0, blocking collectives: 605 us -> none
    all_gather x1 -> x0, waiting for transfers between devices: 572 us -> none  [per_device(): whole_proj = lax.all_gather(group_proj, 'ctx', axis=0, tiled=True)]
    all_to_all x0 -> x4, waiting for transfers between devices: none -> 44.4 us  [the longest x1 27.7 us: gather_columns(): plane = lax.all_to_all(shared(line, NX * NY), ('x', 'ylo'), 0, 0)]
    all_to_all x0 -> x4, starting transfers between devices: none -> 33.9 us  [the longest x1 15.2 us: gather_columns(): line = lax.all_to_all(shared(mine, NZ), 'z', 0, 0)]
    gather x8 -> x0, local copies, waits for them, and re-layouts: 17.5 us -> none  [per_device(): extended[local_index[:, column]].astype(jnp.float32) * weight_entry]
    ppermute x2 -> x4, waiting for transfers between devices: 27.3 us -> 25.5 us  [the longest x1 19.6 us: per_device(): lower = lax.ppermute(teacher_hidden[row_count - HALO:], CTX, up)]
  transfers between devices with their start and end apart: 3 -> 8, of which waited for: 2 -> 7; matrix products, arithmetic and copies ran while one was open for 1% -> 10% of each run, Pallas kernels for 0% -> 0%
where the time goes in v1:
time: 157 us; the launch traced here: 156 us
  waiting for transfers between devices  69.9 us (45%)
  starting transfers between devices  47.9 us (31%)
  other arithmetic  13.6 us (9%)
  local copies, waits for them, and re-layouts  12.6 us (8%)
  matrix products  7.62 us (5%)
  between operations  4.08 us (3%)
    all_to_all x1, waiting for transfers between devices, gather_columns(): plane = lax.all_to_all(shared(line, NX * NY), ('x', 'ylo'), 0, 0)  27.7 us
    ppermute x1, waiting for transfers between devices, per_device(): lower = lax.ppermute(teacher_hidden[row_count - HALO:], CTX, up)  19.6 us
    all_to_all x1, starting transfers between devices, gather_columns(): line = lax.all_to_all(shared(mine, NZ), 'z', 0, 0)  15.2 us
    all_to_all x1, starting transfers between devices, per_device(): terms = jnp.sum(lax.all_to_all(terms, 'z', 0, 0), axis=0)  11.7 us
    all_to_all x1, waiting for transfers between devices, per_device(): terms = jnp.sum(lax.all_to_all(terms, 'z', 0, 0), axis=0)  10.6 us
    ppermute x1, starting transfers between devices, per_device(): upper = lax.ppermute(teacher_hidden[:HALO], CTX, down)  6.87 us
    dot_general x3, matrix products, summed(): jnp.dot(counts(first, rows.shape[0]), normalize(rows, teacher_gain), pref...  6.5 us
    all_to_all x1, waiting for transfers between devices, per_device(): terms = jnp.sum(lax.all_to_all(terms, ('x', 'ylo'), 0, 0), axis=0)  6.11 us
  transfers between devices with their start and end apart: 8, of which 7 were waited for; matrix products, arithmetic and copies ran while one was open for 10% of the time, Pallas kernels for 0%

profile of v1, /device:TPU:16, one launch (start us, length us, event | category | flops | bytes accessed | tf_op | source)
XLA Modules:
  0.0 155.7 jit_solution(2835705813538547110)
XLA Ops:
  0.6 0.0 copy-start
  0.6 0.0 copy-start.1
  0.7 0.8 copy-done
  1.4 0.8 broadcast_in_dim.9
  2.2 15.2 %all-to-all-start = ((bf16[16,40,256]{2,1,0:T(8,128)(2,1)}), bf16[16,40,256]{2,1,0:T(8,128)(2,1)}, u32[]{:S(2)}, u32[]{:S(2)}) async-start(bf16[16,40,256]{2,1,0:T(8,128)(2,1)} %broadcast_in_dim.9), calls=%async_computation | async-start | bytes 655360 | tf_op jit(solution)/shard_map/all_to_all | solution.py:29
  17.4 0.0 copy-start.7
  17.4 0.0 copy-start.6
  17.4 2.4 %fusion.45 = (bf16[64,5120]{1,0:T(8,128)(2,1)}, bf16[64,5120]{1,0:T(8,128)(2,1)}) fusion(bf16[256,5120]{1,0:T(8,128)(2,1)} %param.8), kind=kLoop, calls=%fused_computation.73 | loop fusion | bytes 2621440 | tf_op jit(solution)/shard_map/slice | solution.py:61
  19.9 0.0 copy-start.4
  19.9 3.3 %collective-permute-start = (bf16[64,5120]{1,0:T(8,128)(2,1)}, bf16[64,5120]{1,0:T(8,128)(2,1)}, u32[]{:S(2)}, u32[]{:S(2)}) collective-permute-start(bf16[64,5120]{1,0:T(8,128)(2,1)} %get-tuple-element.9), channel_id=1, source_target_pairs={{0,4},{4,8},{8,12},{12,16},{16,20},{20,24},{24,28},{28,32},{32,36}... | collective-permute-start | bytes 1966088 | tf_op jit(solution)/shard_map/ppermute | solution.py:60
  23.2 6.9 %collective-permute-start.1 = (bf16[64,5120]{1,0:T(8,128)(2,1)}, bf16[64,5120]{1,0:T(8,128)(2,1)S(1)}, u32[]{:S(2)}, u32[]{:S(2)}) collective-permute-start(bf16[64,5120]{1,0:T(8,128)(2,1)} %get-tuple-element.8), channel_id=1, source_target_pairs={{4,0},{8,4},{12,8},{16,12},{20,16},{24,20},{28,24},{32,28},{36,32}... | collective-permute-start | bytes 1966088 | tf_op jit(solution)/shard_map/ppermute | solution.py:61
  30.1 0.0 copy-done.1
  30.1 0.6 fusion.2
  30.7 0.0 copy-done.7
  30.7 0.0 copy-done.6
  30.8 0.1 convert_reduce_fusion.1
  30.9 0.1 copy.34
  31.0 0.4 convert_reduce_fusion
  31.4 0.0 copy-done.4
  31.4 1.0 fusion.9
  32.4 19.6 %collective-permute-done = bf16[64,5120]{1,0:T(8,128)(2,1)} collective-permute-done((bf16[64,5120]{1,0:T(8,128)(2,1)}, bf16[64,5120]{1,0:T(8,128)(2,1)}, u32[]{:S(2)}, u32[]{:S(2)}) %collective-permute-start) | collective-permute-done | bytes 655392 | tf_op jit(solution)/shard_map/ppermute | solution.py:60
  52.0 1.3 fusion.30
  53.3 1.9 %collective-permute-done.1 = bf16[64,5120]{1,0:T(8,128)(2,1)S(1)} collective-permute-done((bf16[64,5120]{1,0:T(8,128)(2,1)}, bf16[64,5120]{1,0:T(8,128)(2,1)S(1)}, u32[]{:S(2)}, u32[]{:S(2)}) %collective-permute-start.1) | collective-permute-done | bytes 655392 | tf_op jit(solution)/shard_map/ppermute | solution.py:61
  55.3 0.2 fusion.33
  55.5 3.2 %convolution_add_fusion.1 = f32[128,5120]{1,0:T(8,128)} fusion(f32[128,5120]{1,0:T(8,128)S(1)} %fusion.9, bf16[64,5120]{1,0:T(8,128)(2,1)} %collective-permute-done, f32[5120]{0:T(1024)S(1)} %copy-done.4, f32[64]{0:T(128)S(1)} %add_rsqrt_fusion.2, bf16[128,64]{0,1:T(8,128)(2,1)S(1)} %get-tuple-element.7), kind=kOutput, calls=%fused_computation.4 | convolution fusion | flops 85852160 | bytes 5935360 | tf_op jit(solution)/shard_map/dot_general | solution.py:76
  58.7 0.0 all-to-all-done
  58.7 2.7 %broadcast_in_dim.10 = bf16[8,16,40,256]{3,2,1,0:T(8,128)(2,1)} broadcast(bf16[16,40,256]{2,1,0:T(8,128)(2,1)} %all-to-all-done), dimensions={1,2,3} | broadcast | bytes 2949120 | tf_op jit(solution)/shard_map/broadcast_in_dim | solution.py:23
  61.3 3.6 %all-to-all-start.1 = ((bf16[8,16,40,256]{3,2,1,0:T(8,128)(2,1)}), bf16[8,16,40,256]{3,2,1,0:T(8,128)(2,1)S(1)}, u32[]{:S(2)}, u32[]{:S(2)}) async-start(bf16[8,16,40,256]{3,2,1,0:T(8,128)(2,1)} %broadcast_in_dim.10), calls=%async_computation.1 | async-start | bytes 5242880 | tf_op jit(solution)/shard_map/all_to_all | solution.py:30
  65.0 2.3 %fusion.1 = bf16[128,5120]{1,0:T(8,128)(2,1)S(1)} fusion(f32[128,5120]{1,0:T(8,128)} %convolution_add_fusion.1, f32[128]{0:T(128)S(1)} %convert_divide_fusion, bf16[64,5120]{1,0:T(8,128)(2,1)S(1)} %collective-permute-done.1, f32[64]{0:T(128)S(1)} %add_rsqrt_fusion.1, f32[5120]{0:T(1024)S(1)} %copy-done.4, bf16[128,64]{0,1:T(8,128)(2,1)S(1)} %get-tuple-element.6), kind=kOutput, calls=%fused_computation.5 | convolution fusion | flops 87162880 | bytes 4625152 | tf_op jit(solution)/shard_map/dot_general | solution.py:76
  67.3 1.9 %collective-permute-start.2 = (bf16[128,5120]{1,0:T(8,128)(2,1)S(1)}, bf16[128,5120]{1,0:T(8,128)(2,1)S(1)}, u32[]{:S(2)}, u32[]{:S(2)}) collective-permute-start(bf16[128,5120]{1,0:T(8,128)(2,1)S(1)} %fusion.1), channel_id=1, source_target_pairs={{0,1},{1,0},{2,3},{3,2},{4,5},{5,4},{6,7},{7,6},{8,9},{9,8},{10,11... | collective-permute-start | bytes 3932168 | tf_op jit(solution)/shard_map/ppermute | solution.py:88
  69.3 3.0 %collective-permute-done.2 = bf16[128,5120]{1,0:T(8,128)(2,1)S(1)} collective-permute-done((bf16[128,5120]{1,0:T(8,128)(2,1)S(1)}, bf16[128,5120]{1,0:T(8,128)(2,1)S(1)}, u32[]{:S(2)}, u32[]{:S(2)}) %collective-permute-start.2) | collective-permute-done | bytes 1310752 | tf_op jit(solution)/shard_map/ppermute | solution.py:88
  72.3 1.7 %pad_maximum_fusion = bf16[256,5120]{1,0:T(8,128)(2,1)} fusion(bf16[128,5120]{1,0:T(8,128)(2,1)S(1)} %collective-permute-done.2, bf16[128,5120]{1,0:T(8,128)(2,1)S(1)} %fusion.1), kind=kLoop, calls=%fused_computation.19 | loop fusion | flops 5242880 | bytes 5242880 | tf_op jit(solution)/shard_map/concatenate | solution.py:89
  73.9 27.7 %all-to-all-done.1 = bf16[8,16,40,256]{3,2,1,0:T(8,128)(2,1)S(1)} async-done(((bf16[8,16,40,256]{3,2,1,0:T(8,128)(2,1)}), bf16[8,16,40,256]{3,2,1,0:T(8,128)(2,1)S(1)}, u32[]{:S(2)}, u32[]{:S(2)}) %all-to-all-start.1) | async-done | bytes 2621472 | tf_op jit(solution)/shard_map/all_to_all | solution.py:30
  101.7 0.0 copy-start.3
  101.7 0.3 copy.33
  102.0 1.5 copy-done.3
  103.4 0.0 copy-start.2
  103.4 1.1 fusion.27
  104.6 0.1 slice.31
  104.7 1.9 %collective-permute-start.3 = (bf16[128,8,256]{0,2,1:T(8,128)(2,1)S(1)}, bf16[128,8,256]{0,2,1:T(8,128)(2,1)S(1)}, u32[]{:S(2)}, u32[]{:S(2)}) collective-permute-start(bf16[128,8,256]{0,2,1:T(8,128)(2,1)S(1)} %slice.31), channel_id=1, source_target_pairs={{0,1},{1,0},{2,3},{3,2},{4,5},{5,4},{6,7},{7,6},{8,9},{9,8},{10,11... | collective-permute-start | bytes 1572872 | tf_op jit(solution)/shard_map/ppermute | solution.py:93
  107.3 0.0 copy-done.2
  107.3 0.3 fusion.23
  107.6 0.9 collective-permute-done.3
  108.5 0.1 broadcast_select_fusion.1
  108.5 0.1 pad_maximum_fusion.1
  108.6 1.6 bitcast_convert_fusion
  110.2 0.0 copy-start.5
  110.2 1.9 %copy.37 = f32[128,4096]{1,0:T(8,128)S(1)} copy(f32[128,4096]{0,1:T(8,128)} %bitcast_convert_fusion) | data formatting | bytes 4194304 | tf_op jit(solution)/shard_map/convert_element_type | solution.py:97
  112.1 0.0 copy-done.5
  112.1 2.1 %multiply_reduce_fusion = (f32[]{:T(128)}, f32[4096]{0:T(1024)S(1)}, f32[128]{0:T(128)S(1)}) fusion(f32[128,4096]{1,0:T(8,128)S(1)} %copy.37, f32[4096]{0:T(1024)S(1)} %copy-done.5, f32[128]{0:T(128)S(1)} %add_rsqrt_fusion.3, bf16[128,4096]{1,0:T(8,128)(2,1)S(1)} %copy-done.2, f32[128]{0:T(128)S(1)} %compare_convert_fusion), kind=kLoop, calls=%fused_computation.30 | loop fusion | flops 6287231 | bytes 3180036 | tf_op jit(solution)/shard_map/reduce_sum | solution.py:110
  114.3 0.1 reshape.83
  114.3 0.7 pad_maximum_fusion.3
  115.1 0.7 reshape.87
  115.8 3.3 %all-to-all-start.2 = ((f32[8,1,544]{2,1,0:T(1,128)}), f32[8,1,544]{2,1,0:T(1,128)S(1)}, u32[]{:S(2)}, u32[]{:S(2)}) async-start(f32[8,1,544]{2,1,0:T(1,128)} %reshape.87), calls=%async_computation.2 | async-start | bytes 40960 | tf_op jit(solution)/shard_map/all_to_all | solution.py:119
  119.2 6.1 %all-to-all-done.2 = f32[8,1,544]{2,1,0:T(1,128)S(1)} async-done(((f32[8,1,544]{2,1,0:T(1,128)}), f32[8,1,544]{2,1,0:T(1,128)S(1)}, u32[]{:S(2)}, u32[]{:S(2)}) %all-to-all-start.2) | async-done | bytes 17440 | tf_op jit(solution)/shard_map/all_to_all | solution.py:119
  125.3 0.5 broadcast.91
  125.8 0.7 reduce.1
  126.5 0.1 reshape.88
  126.6 0.6 reduce_sum.118
  127.2 11.7 %all-to-all-start.3 = ((f32[16,1,34]{2,1,0:T(1,128)}), f32[16,1,34]{2,1,0:T(1,128)S(1)}, u32[]{:S(2)}, u32[]{:S(2)}) async-start(f32[16,1,34]{2,1,0:T(1,128)} %bitcast.7), calls=%async_computation.3 | async-start | bytes 16384 | tf_op jit(solution)/shard_map/all_to_all | solution.py:120
  138.9 1.8 %fusion.21 = bf16[128,4096]{1,0:T(8,128)(2,1)} fusion(bf16[128,4096]{1,0:T(8,128)(2,1)S(1)} %copy-done.2, f32[128]{0:T(128)S(1)} %broadcast_multiply_fusion, f32[4096]{0:T(1024)S(1)} %copy-done.5, f32[128]{0:T(128)S(1)} %add_rsqrt_fusion.3, f32[128,4096]{1,0:T(8,128)S(1)} %copy.37, f32[128]{0:T(128)S(1)} %compare_convert_fusion), kind=kLoop, calls=%fused_computation.27 | loop fusion | flops 5242880 | bytes 4212224 | tf_op jit(solution)/shard_map/convert_element_type | solution.py:108
  140.7 10.6 %all-to-all-done.3 = f32[16,1,34]{2,1,0:T(1,128)S(1)} async-done(((f32[16,1,34]{2,1,0:T(1,128)}), f32[16,1,34]{2,1,0:T(1,128)S(1)}, u32[]{:S(2)}, u32[]{:S(2)}) %all-to-all-start.3) | async-done | bytes 2208 | tf_op jit(solution)/shard_map/all_to_all | solution.py:120
  151.3 0.7 fusion.46
  152.0 1.2 slice_divide_fusion
  (14 shorter events, 0.1 us)
Async XLA Ops:
  0.6 0.8 copy-start
  0.6 29.4 %copy-start.1 = (bf16[256,5120]{1,0:T(8,128)(2,1)S(1)}, bf16[256,5120]{1,0:T(8,128)(2,1)}, u32[]{:S(2)}) copy-start(bf16[256,5120]{1,0:T(8,128)(2,1)} %param.8) | copy-start | bytes 7864324
  2.2 56.5 %all-to-all-start = ((bf16[16,40,256]{2,1,0:T(8,128)(2,1)}), bf16[16,40,256]{2,1,0:T(8,128)(2,1)}, u32[]{:S(2)}, u32[]{:S(2)}) async-start(bf16[16,40,256]{2,1,0:T(8,128)(2,1)} %broadcast_in_dim.9), calls=%async_computation | async-start | bytes 655360 | tf_op jit(solution)/shard_map/all_to_all | solution.py:29
  17.4 13.3 %copy-start.7 = (s32[128]{0:T(128)S(1)}, s32[128]{0:T(128)}, u32[]{:S(2)}) copy-start(s32[128]{0:T(128)} %param.15) | copy-start | bytes 1540
  17.4 13.3 %copy-start.6 = (s32[128,8]{0,1:T(8,128)S(1)}, s32[128,8]{0,1:T(8,128)}, u32[]{:S(2)}) copy-start(s32[128,8]{0,1:T(8,128)} %param.14) | copy-start | bytes 12292
  19.9 11.5 %copy-start.4 = (f32[5120]{0:T(1024)S(1)}, f32[5120]{0:T(1024)}, u32[]{:S(2)}) copy-start(f32[5120]{0:T(1024)} %param.9) | copy-start | bytes 61444
  19.9 32.1 %collective-permute-start = (bf16[64,5120]{1,0:T(8,128)(2,1)}, bf16[64,5120]{1,0:T(8,128)(2,1)}, u32[]{:S(2)}, u32[]{:S(2)}) collective-permute-start(bf16[64,5120]{1,0:T(8,128)(2,1)} %get-tuple-element.9), channel_id=1, source_target_pairs={{0,4},{4,8},{8,12},{12,16},{16,20},{20,24},{24,28},{28,32},{32,36}... | collective-permute-start | bytes 1966088 | tf_op jit(solution)/shard_map/ppermute | solution.py:60
  23.2 32.1 %collective-permute-start.1 = (bf16[64,5120]{1,0:T(8,128)(2,1)}, bf16[64,5120]{1,0:T(8,128)(2,1)S(1)}, u32[]{:S(2)}, u32[]{:S(2)}) collective-permute-start(bf16[64,5120]{1,0:T(8,128)(2,1)} %get-tuple-element.8), channel_id=1, source_target_pairs={{4,0},{8,4},{12,8},{16,12},{20,16},{24,20},{28,24},{32,28},{36,32}... | collective-permute-start | bytes 1966088 | tf_op jit(solution)/shard_map/ppermute | solution.py:61
  61.3 40.3 %all-to-all-start.1 = ((bf16[8,16,40,256]{3,2,1,0:T(8,128)(2,1)}), bf16[8,16,40,256]{3,2,1,0:T(8,128)(2,1)S(1)}, u32[]{:S(2)}, u32[]{:S(2)}) async-start(bf16[8,16,40,256]{3,2,1,0:T(8,128)(2,1)} %broadcast_in_dim.10), calls=%async_computation.1 | async-start | bytes 5242880 | tf_op jit(solution)/shard_map/all_to_all | solution.py:30
  67.3 4.9 %collective-permute-start.2 = (bf16[128,5120]{1,0:T(8,128)(2,1)S(1)}, bf16[128,5120]{1,0:T(8,128)(2,1)S(1)}, u32[]{:S(2)}, u32[]{:S(2)}) collective-permute-start(bf16[128,5120]{1,0:T(8,128)(2,1)S(1)} %fusion.1), channel_id=1, source_target_pairs={{0,1},{1,0},{2,3},{3,2},{4,5},{5,4},{6,7},{7,6},{8,9},{9,8},{10,11... | collective-permute-start | bytes 3932168 | tf_op jit(solution)/shard_map/ppermute | solution.py:88
  101.7 1.7 %copy-start.3 = (bf16[256,5120]{1,0:T(8,128)(2,1)S(1)}, bf16[256,5120]{1,0:T(8,128)(2,1)}, u32[]{:S(2)}) copy-start(bf16[256,5120]{1,0:T(8,128)(2,1)} %pad_maximum_fusion) | copy-start | bytes 7864324
  103.4 3.8 %copy-start.2 = (bf16[128,4096]{1,0:T(8,128)(2,1)S(1)}, bf16[128,4096]{1,0:T(8,128)(2,1)}, u32[]{:S(2)}) copy-start(bf16[128,4096]{1,0:T(8,128)(2,1)} %param.11) | copy-start | bytes 3145732
  104.7 3.8 %collective-permute-start.3 = (bf16[128,8,256]{0,2,1:T(8,128)(2,1)S(1)}, bf16[128,8,256]{0,2,1:T(8,128)(2,1)S(1)}, u32[]{:S(2)}, u32[]{:S(2)}) collective-permute-start(bf16[128,8,256]{0,2,1:T(8,128)(2,1)S(1)} %slice.31), channel_id=1, source_target_pairs={{0,1},{1,0},{2,3},{3,2},{4,5},{5,4},{6,7},{7,6},{8,9},{9,8},{10,11... | collective-permute-start | bytes 1572872 | tf_op jit(solution)/shard_map/ppermute | solution.py:93
  110.2 1.9 %copy-start.5 = (f32[4096]{0:T(1024)S(1)}, f32[4096]{0:T(1024)}, u32[]{:S(2)}) copy-start(f32[4096]{0:T(1024)} %param.12) | copy-start | bytes 49156
  115.8 9.5 %all-to-all-start.2 = ((f32[8,1,544]{2,1,0:T(1,128)}), f32[8,1,544]{2,1,0:T(1,128)S(1)}, u32[]{:S(2)}, u32[]{:S(2)}) async-start(f32[8,1,544]{2,1,0:T(1,128)} %reshape.87), calls=%async_computation.2 | async-start | bytes 40960 | tf_op jit(solution)/shard_map/all_to_all | solution.py:119
  127.2 24.1 %all-to-all-start.3 = ((f32[16,1,34]{2,1,0:T(1,128)}), f32[16,1,34]{2,1,0:T(1,128)S(1)}, u32[]{:S(2)}, u32[]{:S(2)}) async-start(f32[16,1,34]{2,1,0:T(1,128)} %bitcast.7), calls=%async_computation.3 | async-start | bytes 16384 | tf_op jit(solution)/shard_map/all_to_all | solution.py:120

commit v2 on v1

v2 whole, which is shorter than its diff:
```python
import jax
import jax.numpy as jnp
from jax import lax
from jax.experimental import pallas as pl
from jax.experimental.pallas import tpu as pltpu
from jax.sharding import Mesh
from jax.sharding import PartitionSpec as P

HD = 128
SH = 32
KVG = 8
SPAN = 8
TG = 5
SG = 4
HALO = 64
NZ = 16
NX = 4
NY = 2
CTX = ("z", "x", "ylo")
PART = ("yhi", "core")
DEVICES = NZ * NX * NY
SWAP = [(0, 1), (1, 0)]
WIDE = SG * HD
HALF = WIDE // 2
LANES = 128
PIECE = SH * HD // DEVICES


def shared(cells, count):
    return jnp.broadcast_to(cells[None], (count,) + cells.shape)


def gather_columns(group_proj):
    mine = lax.dynamic_slice_in_dim(group_proj, lax.axis_index("core") * HALF, HALF, axis=1)
    line = lax.all_to_all(shared(mine, NZ), "z", 0, 0)
    groups = [[x * 4 + lo * 2 + (lo ^ k) for x in range(NX) for lo in range(NY)] for k in range(2)]
    plane = lax.all_to_all(
        shared(line, NX * NY), ("x", "ylo", "yhi"), 0, 0, axis_index_groups=groups
    )
    return plane.transpose(1, 0, 2, 3).reshape(KVG, TG * HD, HALF), line


def normalize(teacher_hidden, teacher_gain):
    teacher_float = teacher_hidden.astype(jnp.float32)
    teacher_scale = lax.rsqrt(
        jnp.mean(teacher_float * teacher_float, axis=-1, keepdims=True) + 1e-05
    )
    return (teacher_float * teacher_scale * teacher_gain).astype(jnp.bfloat16)


def mismatch_block(group, core_ref, count_ref, student_ref, inv, gain_ref, own_ref, back_ref):
    slots = student_ref.shape[0]
    wide = slice(group * WIDE, (group + 1) * WIDE)
    own = own_ref[group].astype(jnp.float32)
    back = back_ref[group].astype(jnp.float32)
    first = core_ref[0] == 0
    low = jnp.where(first, own, back)
    high = jnp.where(first, back, own)
    pooled = jnp.concatenate([low, high], axis=1)
    normed = student_ref[:, wide].astype(jnp.float32) * inv
    live = lax.broadcasted_iota(jnp.int32, (slots, 1), 0) < count_ref[0]
    gain = gain_ref[:, wide]
    mismatch = jnp.where(live, normed * gain - pooled, 0.0)
    return normed, mismatch, gain


def sums_kernel(
    core_ref, count_ref, student_ref, inv_ref, gain_ref, own_ref, back_ref, terms_ref, inner_ref
):
    slots = student_ref.shape[0]
    inv = inv_ref[...]
    inner = jnp.zeros((slots, LANES), jnp.float32)
    square = jnp.zeros((1, LANES), jnp.float32)
    per = LANES // PIECE
    blocks = []
    for group in range(KVG):
        normed, mismatch, gain = mismatch_block(
            group, core_ref, count_ref, student_ref, inv, gain_ref, own_ref, back_ref
        )
        product = mismatch * normed
        weighted = product * gain
        sums = jnp.sum(product, axis=0, keepdims=True)
        squares = jnp.sum(mismatch * mismatch, axis=0, keepdims=True)
        for tile in range(WIDE // LANES):
            part = slice(tile * LANES, (tile + 1) * LANES)
            inner = inner + weighted[:, part]
            square = square + squares[:, part]
            lanes = sums[:, part]
            for turn in range(per):
                blocks.append(lanes if turn == 0 else pltpu.roll(lanes, LANES - turn * PIECE, 1))
    inner_ref[...] = jnp.sum(inner, axis=1, keepdims=True)
    block = jnp.concatenate(blocks, axis=0)
    lane = lax.broadcasted_iota(jnp.int32, block.shape, 1)
    total = jnp.sum(square, axis=1, keepdims=True)
    live = count_ref[0].astype(jnp.float32)
    block = jnp.where(lane < PIECE, block, 0.0)
    block = jnp.where(lane == PIECE, total, block)
    terms_ref[...] = jnp.where(lane == PIECE + 1, live, block)


def rows_kernel(
    core_ref, count_ref, student_ref, inv_ref, gain_ref, own_ref, back_ref, inner_ref, grad_ref
):
    inv = inv_ref[...]
    mean = inner_ref[...] * (1.0 / (SH * HD))
    for group in range(KVG):
        normed, mismatch, gain = mismatch_block(
            group, core_ref, count_ref, student_ref, inv, gain_ref, own_ref, back_ref
        )
        grad = inv * (mismatch * gain - normed * mean)
        grad_ref[:, group * WIDE : (group + 1) * WIDE] = grad.astype(grad_ref.dtype)


def per_device(
    teacher_hidden,
    teacher_gain,
    group_proj,
    student_hidden,
    student_gain,
    student_count,
    spans,
    span_len,
):
    row_count = teacher_hidden.shape[0]
    slot_count = student_hidden.shape[0]
    core = lax.axis_index("core")
    lo = lax.axis_index("ylo")

    within = [(i, i ^ 1) for i in range(DEVICES)]
    across = [(i, (i + 1 if i % 2 else i - 1) % DEVICES) for i in range(DEVICES)]
    head = teacher_hidden[:HALO]
    tail = teacher_hidden[row_count - HALO :]
    inner = lax.ppermute(jnp.where(lo == 0, tail, head), CTX, within)
    outer = lax.ppermute(jnp.where(lo == 0, head, tail), CTX, across)

    weights, line = gather_columns(group_proj)
    teacher_hidden = lax.optimization_barrier((teacher_hidden, line))[0]
    inner = lax.optimization_barrier((inner, line))[0]
    outer = lax.optimization_barrier((outer, line))[0]

    offset_rows = lax.axis_index(CTX) * row_count - HALO
    local_index = spans - offset_rows
    live_entry = jnp.arange(SPAN, dtype=jnp.int32)[None, :] < span_len[:, None]
    local_index = jnp.where(live_entry, local_index, -1)

    def counts(first, rows):
        wanted = jnp.arange(rows, dtype=jnp.int32) + first
        hits = local_index[:, :, None] == wanted[None, None, :]
        return jnp.sum(hits.astype(jnp.float32), axis=1).astype(jnp.bfloat16)

    def summed(first, rows):
        return jnp.dot(
            counts(first, rows.shape[0]),
            normalize(rows, teacher_gain),
            preferred_element_type=jnp.float32,
        )

    total = summed(HALO, teacher_hidden)
    total = total + summed(jnp.where(lo == 0, HALO + row_count, 0), inner)
    total = total + summed(jnp.where(lo == 0, 0, HALO + row_count), outer)
    share = 1.0 / jnp.maximum(span_len, 1).astype(jnp.float32)[:, None]
    pooled_normed = (total * share).astype(jnp.bfloat16)

    other_normed = lax.ppermute(pooled_normed, "core", SWAP)
    pooled_normed = pooled_normed.reshape(slot_count, KVG, TG * HD)
    other_normed = other_normed.reshape(slot_count, KVG, TG * HD)

    def projected(rows):
        mixed = jnp.einsum("rgk,gkm->grm", rows, weights, preferred_element_type=jnp.float32)
        return mixed.astype(jnp.bfloat16)

    back = lax.ppermute(projected(other_normed), "core", SWAP)
    own = projected(pooled_normed)

    student_float = student_hidden.astype(jnp.float32)
    inv_rms = lax.rsqrt(jnp.mean(student_float * student_float, axis=-1, keepdims=True) + 1e-05)
    operands = (
        core.astype(jnp.int32).reshape(1),
        student_count,
        student_hidden,
        inv_rms,
        student_gain.reshape(1, SH * HD),
        own,
        back,
    )
    scalar = pl.BlockSpec(memory_space=pltpu.SMEM)
    whole = pl.BlockSpec(memory_space=pltpu.VMEM)
    limit = pltpu.CompilerParams(vmem_limit_bytes=32 * 1024 * 1024)
    terms, inner_sum = pl.pallas_call(
        sums_kernel,
        in_specs=[scalar, scalar] + [whole] * 5,
        out_specs=[whole, whole],
        out_shape=[
            jax.ShapeDtypeStruct((DEVICES, LANES), jnp.float32),
            jax.ShapeDtypeStruct((slot_count, 1), jnp.float32),
        ],
        compiler_params=limit,
        cost_estimate=pl.CostEstimate(flops=8_000_000, bytes_accessed=2_200_000, transcendentals=0),
    )(*operands)
    grad_rows = pl.pallas_call(
        rows_kernel,
        in_specs=[scalar, scalar] + [whole] * 6,
        out_specs=whole,
        out_shape=jax.ShapeDtypeStruct((slot_count, SH * HD), jnp.bfloat16),
        compiler_params=limit,
        cost_estimate=pl.CostEstimate(flops=8_000_000, bytes_accessed=3_200_000, transcendentals=0),
    )(*operands, inner_sum)

    terms = jnp.sum(lax.all_to_all(terms, CTX, 0, 0, tiled=True), axis=0)
    live_total = terms[PIECE + 1]
    grad_gain = terms[:PIECE] / live_total
    loss = (terms[PIECE] / (SH * HD * live_total)).reshape(1)
    return (grad_rows, grad_gain, loss)


def solution(mesh):
    fine = Mesh(mesh.devices.reshape(NZ, NX, NY, 2, 2), CTX + PART)
    every = PART + CTX
    placed = (
        P(every, None),
        P(),
        P(CTX, None),
        P(every, None),
        P(),
        P(every),
        P(every, None),
        P(every),
    )
    return jax.shard_map(
        per_device,
        mesh=fine,
        in_specs=placed,
        out_specs=(P(every, None), P(every), P(PART)),
        check_vma=False,
    )
```

time: 157 us -> 126 us (0.80)
  waiting for transfers between devices: 69.9 us -> 44.4 us
  other arithmetic: 13.6 us -> 6.77 us
  local copies, waits for them, and re-layouts: 12.6 us -> 6.05 us
  Pallas kernels: 0 us -> 4.02 us
  starting transfers between devices: 47.9 us -> 51.1 us
  matrix products: 7.62 us -> 9.35 us
    ppermute x3, waiting for transfers between devices: 22.5 us -> 7.43 us  [the longest x1 4.78 us: per_device(): inner = lax.ppermute(jnp.where(lo == 0, tail, head), CTX, within)]
    all_to_all x3 -> x2, waiting for transfers between devices: 44.4 us -> 30 us  [the longest x1 17 us: gather_columns(): lax.all_to_all(shared(line, NX * NY), ('x', 'ylo', 'yhi'), 0, 0, axis_ind...]
    all_to_all x1, waiting for transfers between devices: 0.01 us -> 6.98 us  [gather_columns(): line = lax.all_to_all(shared(mine, NZ), 'z', 0, 0)]
    dot_general x1 -> x2, matrix products: 1.12 us -> 6.02 us  [projected(): jnp.einsum('rgk,gkm->grm', rows, weights, preferred_element_type=jnp.floa...]
    pallas_call x0 -> x2, Pallas kernels: none -> 4.02 us  [the longest x1 2.17 us: per_device(): pl.pallas_call(rows_kernel, in_specs=[scalar, scalar] + [whole] * 6, out_...]
    convert_element_type x3 -> x0, other arithmetic: 3.36 us -> none  [the longest x1 1.8 us: per_device(): (inv_rms * (scaled - normed_student * inner_mean)).astype(jnp.bfloat16)]
    dot_general x3, matrix products: 6.5 us -> 3.32 us  [summed(): jnp.dot(counts(first, rows.shape[0]), normalize(rows, teacher_gain), pref...]
    ppermute x1, waiting for transfers between devices: 3 us -> 0.01 us  [per_device(): other_normed = lax.ppermute(pooled_normed, 'core', SWAP)]
  transfers between devices with their start and end apart: 8 -> 7, of which waited for: 7 -> 5; matrix products, arithmetic and copies ran while one was open for 10% -> 12% of each run, Pallas kernels for 0% -> 2%
where the time goes in v2:
time: 126 us
  starting transfers between devices  51.1 us (41%)
  waiting for transfers between devices  44.4 us (35%)
  matrix products  9.35 us (7%)
  other arithmetic  6.77 us (5%)
  local copies, waits for them, and re-layouts  6.05 us (5%)
  Pallas kernels  4.02 us (3%)
  between operations  4.01 us (3%)
    all_to_all x1, waiting for transfers between devices, gather_columns(): lax.all_to_all(shared(line, NX * NY), ('x', 'ylo', 'yhi'), 0, 0, axis_ind...  17 us
    all_to_all x1, starting transfers between devices, gather_columns(): line = lax.all_to_all(shared(mine, NZ), 'z', 0, 0)  15.2 us
    all_to_all x1, starting transfers between devices, per_device(): terms = jnp.sum(lax.all_to_all(terms, CTX, 0, 0, tiled=True), axis=0)  14.9 us
    all_to_all x1, waiting for transfers between devices, per_device(): terms = jnp.sum(lax.all_to_all(terms, CTX, 0, 0, tiled=True), axis=0)  13 us
    ppermute x1, starting transfers between devices, per_device(): outer = lax.ppermute(jnp.where(lo == 0, head, tail), CTX, across)  7.42 us
    all_to_all x1, waiting for transfers between devices, gather_columns(): line = lax.all_to_all(shared(mine, NZ), 'z', 0, 0)  6.98 us
    all_to_all x1, starting transfers between devices, gather_columns(): lax.all_to_all(shared(line, NX * NY), ('x', 'ylo', 'yhi'), 0, 0, axis_ind...  6.44 us
    dot_general x2, matrix products, projected(): jnp.einsum('rgk,gkm->grm', rows, weights, preferred_element_type=jnp.floa...  6.02 us
  transfers between devices with their start and end apart: 7, of which 5 were waited for; matrix products, arithmetic and copies ran while one was open for 12% of the time, Pallas kernels for 2%

profile of v2, /device:TPU:16, one launch (start us, length us, event | category | flops | bytes accessed | tf_op | source)
XLA Modules:
  0.0 125.7 jit_solution(17802799794775439041)
XLA Ops:
  0.6 0.0 copy-start
  0.6 0.0 copy-start.8
  0.7 0.0 copy-start.9
  0.7 0.7 copy-done
  1.4 0.7 broadcast_in_dim.8
  2.2 15.2 %all-to-all-start = ((bf16[16,40,256]{2,1,0:T(8,128)(2,1)}), bf16[16,40,256]{2,1,0:T(8,128)(2,1)S(1)}, u32[]{:S(2)}, u32[]{:S(2)}) async-start(bf16[16,40,256]{2,1,0:T(8,128)(2,1)} %broadcast_in_dim.8), calls=%async_computation | async-start | bytes 655360 | tf_op jit(solution)/shard_map/all_to_all | solution.py:35
  17.4 2.5 %broadcast_select_fusion = (bf16[64,5120]{1,0:T(8,128)(2,1)}, bf16[64,5120]{1,0:T(8,128)(2,1)}) fusion(pred[]{:T(512)S(6)} %eq.22, bf16[256,5120]{1,0:T(8,128)(2,1)} %param.8), kind=kLoop, calls=%fused_computation.36 | loop fusion | flops 655360 | bytes 2621441 | tf_op jit(solution)/shard_map/jit(_where)/select_n | solution.py:134
  19.8 3.2 %collective-permute-start = (bf16[64,5120]{1,0:T(8,128)(2,1)}, bf16[64,5120]{1,0:T(8,128)(2,1)}, u32[]{:S(2)}, u32[]{:S(2)}) collective-permute-start(bf16[64,5120]{1,0:T(8,128)(2,1)} %get-tuple-element.16), channel_id=1, source_target_pairs={{0,4},{4,0},{8,12},{12,8},{16,20},{20,16},{24,28},{28,24},{32,36},... | collective-permute-start | bytes 1966088 | tf_op jit(solution)/shard_map/ppermute | solution.py:133
  23.0 7.4 %collective-permute-start.1 = (bf16[64,5120]{1,0:T(8,128)(2,1)}, bf16[64,5120]{1,0:T(8,128)(2,1)S(1)}, u32[]{:S(2)}, u32[]{:S(2)}) collective-permute-start(bf16[64,5120]{1,0:T(8,128)(2,1)} %get-tuple-element.15), channel_id=1, source_target_pairs={{0,508},{4,8},{8,4},{12,16},{16,12},{20,24},{24,20},{28,32},{32,28... | collective-permute-start | bytes 1966088 | tf_op jit(solution)/shard_map/ppermute | solution.py:134
  30.5 0.0 copy-done.8
  30.5 0.0 copy-done.9
  30.5 0.1 copy.25
  30.6 0.1 convert_reduce_fusion.1
  30.7 0.4 convert_reduce_fusion
  31.2 7.0 %all-to-all-done = bf16[16,40,256]{2,1,0:T(8,128)(2,1)S(1)} async-done(((bf16[16,40,256]{2,1,0:T(8,128)(2,1)}), bf16[16,40,256]{2,1,0:T(8,128)(2,1)S(1)}, u32[]{:S(2)}, u32[]{:S(2)}) %all-to-all-start) | async-done | bytes 327712 | tf_op jit(solution)/shard_map/all_to_all | solution.py:35
  38.1 1.7 %broadcast_in_dim.9 = bf16[8,16,40,256]{3,2,1,0:T(8,128)(2,1)} broadcast(bf16[16,40,256]{2,1,0:T(8,128)(2,1)S(1)} %all-to-all-done), dimensions={1,2,3} | broadcast | bytes 2949120 | tf_op jit(solution)/shard_map/broadcast_in_dim | solution.py:30
  39.8 0.0 copy-start.4
  39.8 6.4 %all-to-all-start.1 = ((bf16[8,16,40,256]{3,2,1,0:T(8,128)(2,1)}), bf16[8,16,40,256]{3,2,1,0:T(8,128)(2,1)}, u32[]{:S(2)}, u32[]{:S(2)}) async-start(bf16[8,16,40,256]{3,2,1,0:T(8,128)(2,1)} %broadcast_in_dim.9), calls=%async_computation.1 | async-start | bytes 5242880 | tf_op jit(solution)/shard_map/all_to_all | solution.py:37
  46.3 0.0 copy-start.7
  46.3 4.8 %collective-permute-done = bf16[64,5120]{1,0:T(8,128)(2,1)} collective-permute-done((bf16[64,5120]{1,0:T(8,128)(2,1)}, bf16[64,5120]{1,0:T(8,128)(2,1)}, u32[]{:S(2)}, u32[]{:S(2)}) %collective-permute-start) | collective-permute-done | bytes 655392 | tf_op jit(solution)/shard_map/ppermute | solution.py:133
  51.1 1.3 %fusion.9 = f32[64]{0:T(128)S(1)} fusion(bf16[64,5120]{1,0:T(8,128)(2,1)} %collective-permute-done), kind=kLoop, calls=%fused_computation.17 | loop fusion | flops 982976 | bytes 655616 | tf_op jit(solution)/shard_map/reduce_sum | solution.py:46
  52.4 0.0 copy-done.4
  52.4 0.6 fusion.2
  53.0 2.6 %collective-permute-done.1 = bf16[64,5120]{1,0:T(8,128)(2,1)S(1)} collective-permute-done((bf16[64,5120]{1,0:T(8,128)(2,1)}, bf16[64,5120]{1,0:T(8,128)(2,1)S(1)}, u32[]{:S(2)}, u32[]{:S(2)}) %collective-permute-start.1) | collective-permute-done | bytes 655392 | tf_op jit(solution)/shard_map/ppermute | solution.py:134
  55.7 0.0 copy-done.7
  55.7 0.0 copy-start.5
  55.7 1.0 fusion.5
  56.7 0.0 copy-done.5
  56.7 0.2 fusion.12
  56.9 0.0 copy-start.6
  56.9 1.7 %convolution_add_fusion.1 = f32[128,5120]{1,0:T(8,128)S(1)} fusion(f32[128,5120]{1,0:T(8,128)S(1)} %fusion.5, bf16[64,5120]{1,0:T(8,128)(2,1)} %collective-permute-done, f32[5120]{0:T(1024)S(1)} %copy-done.7, f32[64]{0:T(128)S(1)} %add_rsqrt_fusion.2, bf16[128,64]{0,1:T(8,128)(2,1)S(1)} %get-tuple-element.14), kind=kOutput, calls=%fused_computation.4 | convolution fusion | flops 85852160 | bytes 5935360 | tf_op jit(solution)/shard_map/dot_general | solution.py:152
  58.7 0.0 copy-start.1
  58.7 0.0 copy-done.6
  58.7 0.6 fusion.1
  59.3 1.9 %collective-permute-start.2 = (bf16[128,5120]{1,0:T(8,128)(2,1)S(1)}, bf16[128,5120]{1,0:T(8,128)(2,1)}, u32[]{:S(2)}, u32[]{:S(2)}) collective-permute-start(bf16[128,5120]{1,0:T(8,128)(2,1)S(1)} %fusion.1), channel_id=1, source_target_pairs={{0,1},{1,0},{2,3},{3,2},{4,5},{5,4},{6,7},{7,6},{8,9},{9,8},{10,11... | collective-permute-start | bytes 3932168 | tf_op jit(solution)/shard_map/ppermute | solution.py:164
  61.9 0.0 copy-done.1
  61.9 0.3 multiply_reduce_fusion
  62.2 17.0 %all-to-all-done.1 = bf16[8,16,40,256]{3,2,1,0:T(8,128)(2,1)} async-done(((bf16[8,16,40,256]{3,2,1,0:T(8,128)(2,1)}), bf16[8,16,40,256]{3,2,1,0:T(8,128)(2,1)}, u32[]{:S(2)}, u32[]{:S(2)}) %all-to-all-start.1) | async-done | bytes 2621472 | tf_op jit(solution)/shard_map/all_to_all | solution.py:37
  79.2 2.0 %copy.26 = bf16[16,8,40,256]{3,2,1,0:T(8,128)(2,1)S(1)} copy(bf16[16,8,40,256]{3,2,0,1:T(8,128)(2,1)} %bitcast.3) | data formatting | bytes 5242880 | tf_op jit(solution)/shard_map/transpose | solution.py:40
  81.2 0.0 copy-start.3
  81.2 0.0 collective-permute-done.2
  81.2 3.7 %fusion.24 = bf16[8,128,256]{2,1,0:T(8,128)(2,1)} fusion(bf16[8,640,256]{2,1,0:T(8,128)(2,1)S(1)} %bitcast.31, bf16[16,8,8,640]{3,2,1,0:T(8,128)(2,1)} %bitcast.13), kind=kOutput, calls=%fused_computation.30 | convolution fusion | flops 335806464 | bytes 4456448 | tf_op jit(solution)/shard_map/rgk,gkm->grm/dot_general | solution.py:169
  84.9 0.0 copy-start.2
  84.9 2.0 %collective-permute-start.3 = (bf16[8,128,256]{2,1,0:T(8,128)(2,1)}, bf16[8,128,256]{2,1,0:T(8,128)(2,1)S(1)}, u32[]{:S(2)}, u32[]{:S(2)}) collective-permute-start(bf16[8,128,256]{2,1,0:T(8,128)(2,1)} %fusion.24), channel_id=1, source_target_pairs={{0,1},{1,0},{2,3},{3,2},{4,5},{5,4},{6,7},{7,6},{8,9},{9,8},{10,11... | collective-permute-start | bytes 1572872 | tf_op jit(solution)/shard_map/ppermute | solution.py:172
  86.9 0.0 copy-done.3
  87.0 0.1 copy.30.inv_ref
  87.1 2.4 %fusion.21.own_ref = bf16[8,128,256]{2,1,0:T(8,128)(2,1)S(1)} fusion(bf16[8,640,256]{2,1,0:T(8,128)(2,1)} %bitcast.32, bf16[16,8,8,640]{3,2,1,0:T(8,128)(2,1)S(1)} %bitcast.33), kind=kOutput, calls=%fused_computation.29 | convolution fusion | flops 335806464 | bytes 4456448 | tf_op jit(solution)/shard_map/rgk,gkm->grm/dot_general | solution.py:169
  89.4 0.0 collective-permute-done.3.back_ref
  89.4 0.0 copy-done.2
  89.5 1.9 %shard_map.103 = (f32[128,128]{1,0:T(8,128)}, f32[128,1]{1,0:T(8,128)S(1)}) custom-call(s32[1]{0:T(128)} %bitcast.core_ref, s32[1]{0:T(128)S(6)} %copy.46.count_ref, bf16[128,4096]{1,0:T(8,128)(2,1)S(1)} %copy-done.1, f32[128,1]{1,0:T(8,128)S(1)} %copy.30.inv_ref, f32[1,4096]{1,0:T(1,128)S(1)} %bitcast.29, bf16[8,128,256]{2,1,0:T(8,128)(2,1)S(1)} %fusion.21.own_ref, ...), custom_call_target="tpu_custom_call" | custom-call | flops 8000000 | bytes 2200000 | tf_op jit(solution)/shard_map/pallas_call | solution.py:189
  91.3 14.9 %all-to-all-start.2 = ((f32[128,1,128]{2,1,0:T(1,128)}), f32[128,1,128]{2,1,0:T(1,128)S(1)}, u32[]{:S(2)}, u32[]{:S(2)}) async-start(f32[128,1,128]{2,1,0:T(1,128)} %bitcast.6), calls=%async_computation.2 | async-start | bytes 131072 | tf_op jit(solution)/shard_map/all_to_all | solution.py:209
  106.2 2.2 %shard_map.104 = bf16[128,4096]{1,0:T(8,128)(2,1)} custom-call(s32[1]{0:T(128)} %bitcast.core_ref, s32[1]{0:T(128)S(6)} %copy.46.count_ref, bf16[128,4096]{1,0:T(8,128)(2,1)S(1)} %copy-done.1, f32[128,1]{1,0:T(8,128)S(1)} %copy.30.inv_ref, f32[1,4096]{1,0:T(1,128)S(1)} %bitcast.30, bf16[8,128,256]{2,1,0:T(8,128)(2,1)S(1)} %fusion.21.own_ref, ...), custom_call_target="tpu_custom_call" | custom-call | flops 8000000 | bytes 3200000 | tf_op jit(solution)/shard_map/pallas_call | solution.py:200
  108.4 13.0 %all-to-all-done.2 = f32[128,1,128]{2,1,0:T(1,128)S(1)} async-done(((f32[128,1,128]{2,1,0:T(1,128)}), f32[128,1,128]{2,1,0:T(1,128)S(1)}, u32[]{:S(2)}, u32[]{:S(2)}) %all-to-all-start.2) | async-done | bytes 65568 | tf_op jit(solution)/shard_map/all_to_all | solution.py:209
  121.4 0.2 reduce_sum.79
  121.5 0.6 fusion.36
  122.1 1.2 slice_divide_fusion
  (9 shorter events, 0.1 us)
Async XLA Ops:
  0.6 0.8 copy-start
  0.6 29.8 %copy-start.8 = (s32[128,8]{0,1:T(8,128)S(1)}, s32[128,8]{0,1:T(8,128)}, u32[]{:S(2)}) copy-start(s32[128,8]{0,1:T(8,128)} %param.14) | copy-start | bytes 12292
  0.7 29.8 %copy-start.9 = (s32[128]{0:T(128)S(1)}, s32[128]{0:T(128)}, u32[]{:S(2)}) copy-start(s32[128]{0:T(128)} %param.15) | copy-start | bytes 1540
  2.2 36.0 %all-to-all-start = ((bf16[16,40,256]{2,1,0:T(8,128)(2,1)}), bf16[16,40,256]{2,1,0:T(8,128)(2,1)S(1)}, u32[]{:S(2)}, u32[]{:S(2)}) async-start(bf16[16,40,256]{2,1,0:T(8,128)(2,1)} %broadcast_in_dim.8), calls=%async_computation | async-start | bytes 655360 | tf_op jit(solution)/shard_map/all_to_all | solution.py:35
  19.8 31.2 %collective-permute-start = (bf16[64,5120]{1,0:T(8,128)(2,1)}, bf16[64,5120]{1,0:T(8,128)(2,1)}, u32[]{:S(2)}, u32[]{:S(2)}) collective-permute-start(bf16[64,5120]{1,0:T(8,128)(2,1)} %get-tuple-element.16), channel_id=1, source_target_pairs={{0,4},{4,0},{8,12},{12,8},{16,20},{20,16},{24,28},{28,24},{32,36},... | collective-permute-start | bytes 1966088 | tf_op jit(solution)/shard_map/ppermute | solution.py:133
  23.0 32.6 %collective-permute-start.1 = (bf16[64,5120]{1,0:T(8,128)(2,1)}, bf16[64,5120]{1,0:T(8,128)(2,1)S(1)}, u32[]{:S(2)}, u32[]{:S(2)}) collective-permute-start(bf16[64,5120]{1,0:T(8,128)(2,1)} %get-tuple-element.15), channel_id=1, source_target_pairs={{0,508},{4,8},{8,4},{12,16},{16,12},{20,24},{24,20},{28,32},{32,28... | collective-permute-start | bytes 1966088 | tf_op jit(solution)/shard_map/ppermute | solution.py:134
  39.8 12.6 %copy-start.4 = (bf16[256,5120]{1,0:T(8,128)(2,1)S(1)}, bf16[256,5120]{1,0:T(8,128)(2,1)}, u32[]{:S(2)}) copy-start(bf16[256,5120]{1,0:T(8,128)(2,1)} %param.8) | copy-start | bytes 7864324
  39.8 39.4 %all-to-all-start.1 = ((bf16[8,16,40,256]{3,2,1,0:T(8,128)(2,1)}), bf16[8,16,40,256]{3,2,1,0:T(8,128)(2,1)}, u32[]{:S(2)}, u32[]{:S(2)}) async-start(bf16[8,16,40,256]{3,2,1,0:T(8,128)(2,1)} %broadcast_in_dim.9), calls=%async_computation.1 | async-start | bytes 5242880 | tf_op jit(solution)/shard_map/all_to_all | solution.py:37
  46.3 9.4 %copy-start.7 = (f32[5120]{0:T(1024)S(1)}, f32[5120]{0:T(1024)}, u32[]{:S(2)}) copy-start(f32[5120]{0:T(1024)} %param.9) | copy-start | bytes 61444
  55.7 1.0 copy-start.5
  56.9 1.8 %copy-start.6 = (bf16[64,5120]{1,0:T(8,128)(2,1)S(1)}, bf16[64,5120]{1,0:T(8,128)(2,1)}, u32[]{:S(2)}) copy-start(bf16[64,5120]{1,0:T(8,128)(2,1)} %copy-done.5) | copy-start | bytes 1966084
  58.7 3.2 %copy-start.1 = (bf16[128,4096]{1,0:T(8,128)(2,1)S(1)}, bf16[128,4096]{1,0:T(8,128)(2,1)}, u32[]{:S(2)}) copy-start(bf16[128,4096]{1,0:T(8,128)(2,1)} %student_ref.3) | copy-start | bytes 3145732
  59.3 21.9 %collective-permute-start.2 = (bf16[128,5120]{1,0:T(8,128)(2,1)S(1)}, bf16[128,5120]{1,0:T(8,128)(2,1)}, u32[]{:S(2)}, u32[]{:S(2)}) collective-permute-start(bf16[128,5120]{1,0:T(8,128)(2,1)S(1)} %fusion.1), channel_id=1, source_target_pairs={{0,1},{1,0},{2,3},{3,2},{4,5},{5,4},{6,7},{7,6},{8,9},{9,8},{10,11... | collective-permute-start | bytes 3932168 | tf_op jit(solution)/shard_map/ppermute | solution.py:164
  81.2 5.7 %copy-start.3 = (bf16[16,8,40,256]{3,2,1,0:T(8,128)(2,1)}, bf16[16,8,40,256]{3,2,1,0:T(8,128)(2,1)S(1)}, u32[]{:S(2)}) copy-start(bf16[16,8,40,256]{3,2,1,0:T(8,128)(2,1)S(1)} %copy.26) | copy-start | bytes 7864324
  84.9 4.6 %copy-start.2 = (f32[4096]{0:T(1024)S(1)}, f32[4096]{0:T(1024)}, u32[]{:S(2)}) copy-start(f32[4096]{0:T(1024)} %param.12) | copy-start | bytes 49156
  84.9 4.6 %collective-permute-start.3 = (bf16[8,128,256]{2,1,0:T(8,128)(2,1)}, bf16[8,128,256]{2,1,0:T(8,128)(2,1)S(1)}, u32[]{:S(2)}, u32[]{:S(2)}) collective-permute-start(bf16[8,128,256]{2,1,0:T(8,128)(2,1)} %fusion.24), channel_id=1, source_target_pairs={{0,1},{1,0},{2,3},{3,2},{4,5},{5,4},{6,7},{7,6},{8,9},{9,8},{10,11... | collective-permute-start | bytes 1572872 | tf_op jit(solution)/shard_map/ppermute | solution.py:172
  91.3 30.0 %all-to-all-start.2 = ((f32[128,1,128]{2,1,0:T(1,128)}), f32[128,1,128]{2,1,0:T(1,128)S(1)}, u32[]{:S(2)}, u32[]{:S(2)}) async-start(f32[128,1,128]{2,1,0:T(1,128)} %bitcast.6), calls=%async_computation.2 | async-start | bytes 131072 | tf_op jit(solution)/shard_map/all_to_all | solution.py:209

commit v3 on v2

--- a/solution.py
+++ b/solution.py
@@ -111,6 +111,13 @@
         grad_ref[:, group * WIDE : (group + 1) * WIDE] = grad.astype(grad_ref.dtype)
 
 
+def total_kernel(terms_ref, grad_ref, loss_ref):
+    total = jnp.sum(terms_ref[...], axis=0)
+    live = jnp.sum(terms_ref[:, PIECE + 1 : PIECE + 2])
+    grad_ref[...] = total[:PIECE] / live
+    loss_ref[...] = total[PIECE : PIECE + 1] / (SH * HD * live)
+
+
 def per_device(
     teacher_hidden,
     teacher_gain,
@@ -127,7 +134,7 @@
     lo = lax.axis_index("ylo")
 
     within = [(i, i ^ 1) for i in range(DEVICES)]
-    across = [(i, (i + 1 if i % 2 else i - 1) % DEVICES) for i in range(DEVICES)]
+    across = [(i, i + 1 if i % 2 else i - 1) for i in range(1, DEVICES - 1)]
     head = teacher_hidden[:HALO]
     tail = teacher_hidden[row_count - HALO :]
     inner = lax.ppermute(jnp.where(lo == 0, tail, head), CTX, within)
@@ -206,10 +213,16 @@
         cost_estimate=pl.CostEstimate(flops=8_000_000, bytes_accessed=3_200_000, transcendentals=0),
     )(*operands, inner_sum)
 
-    terms = jnp.sum(lax.all_to_all(terms, CTX, 0, 0, tiled=True), axis=0)
-    live_total = terms[PIECE + 1]
-    grad_gain = terms[:PIECE] / live_total
-    loss = (terms[PIECE] / (SH * HD * live_total)).reshape(1)
+    terms = lax.all_to_all(terms, CTX, 0, 0, tiled=True)
+    grad_gain, loss = pl.pallas_call(
+        total_kernel,
+        in_specs=[whole],
+        out_specs=[whole, whole],
+        out_shape=[
+            jax.ShapeDtypeStruct((PIECE,), jnp.float32),
+            jax.ShapeDtypeStruct((1,), jnp.float32),
+        ],
+    )(terms)
     return (grad_rows, grad_gain, loss)
 
 

time: 126 us -> 124 us (0.984)
  starting transfers between devices: 51.1 us -> 46.3 us
  waiting for transfers between devices: 44.4 us -> 49.2 us
  between operations: 4.01 us -> 1.61 us
  Pallas kernels: 4.02 us -> 5.65 us
  other arithmetic: 6.77 us -> 5.49 us
    ppermute x1, starting transfers between devices: 7.42 us -> 0.7 us  [per_device(): outer = lax.ppermute(jnp.where(lo == 0, head, tail), CTX, across)]
    all_to_all x1, waiting for transfers between devices: 6.98 us -> 13.7 us  [gather_columns(): line = lax.all_to_all(shared(mine, NZ), 'z', 0, 0)]
    ppermute x1, waiting for transfers between devices: 2.65 us -> 0.01 us  [per_device(): outer = lax.ppermute(jnp.where(lo == 0, head, tail), CTX, across)]
    all_to_all x1, starting transfers between devices: 14.9 us -> 16.8 us  [per_device(): terms = lax.all_to_all(terms, CTX, 0, 0, tiled=True)]
    pallas_call x0 -> x1, Pallas kernels: none -> 1.63 us  [per_device(): pl.pallas_call(total_kernel, in_specs=[whole], out_specs=[whole, whole],...]
  transfers between devices with their start and end apart: 7 -> 7, of which waited for: 5 -> 4; matrix products, arithmetic and copies ran while one was open for 12% -> 12% of each run, Pallas kernels for 2% -> 2%
where the time goes in v3:
time: 124 us
  waiting for transfers between devices  49.2 us (40%)
  starting transfers between devices  46.3 us (37%)
  matrix products  9.34 us (8%)
  local copies, waits for them, and re-layouts  6.03 us (5%)
  Pallas kernels  5.65 us (5%)
  other arithmetic  5.49 us (4%)
  between operations  1.61 us (1%)
    all_to_all x1, waiting for transfers between devices, gather_columns(): lax.all_to_all(shared(line, NX * NY), ('x', 'ylo', 'yhi'), 0, 0, axis_ind...  17.8 us
    all_to_all x1, starting transfers between devices, per_device(): terms = lax.all_to_all(terms, CTX, 0, 0, tiled=True)  16.8 us
    all_to_all x1, starting transfers between devices, gather_columns(): line = lax.all_to_all(shared(mine, NZ), 'z', 0, 0)  15.2 us
    all_to_all x1, waiting for transfers between devices, gather_columns(): line = lax.all_to_all(shared(mine, NZ), 'z', 0, 0)  13.7 us
    all_to_all x1, waiting for transfers between devices, per_device(): terms = lax.all_to_all(terms, CTX, 0, 0, tiled=True)  13 us
    all_to_all x1, starting transfers between devices, gather_columns(): lax.all_to_all(shared(line, NX * NY), ('x', 'ylo', 'yhi'), 0, 0, axis_ind...  6.53 us
    dot_general x2, matrix products, projected(): jnp.einsum('rgk,gkm->grm', rows, weights, preferred_element_type=jnp.floa...  6.02 us
    ppermute x1, waiting for transfers between devices, per_device(): inner = lax.ppermute(jnp.where(lo == 0, tail, head), CTX, within)  4.73 us
  transfers between devices with their start and end apart: 7, of which 4 were waited for; matrix products, arithmetic and copies ran while one was open for 12% of the time, Pallas kernels for 2%

profile of v3, /device:TPU:16, one launch (start us, length us, event | category | flops | bytes accessed | tf_op | source)
XLA Modules:
  0.0 123.6 jit_solution(14865738651269927790)
XLA Ops:
  0.6 0.0 copy-start
  0.6 0.0 copy-start.9
  0.7 0.0 copy-start.10
  0.7 0.7 copy-done
  1.4 0.7 broadcast_in_dim.8
  2.2 15.2 %all-to-all-start = ((bf16[16,40,256]{2,1,0:T(8,128)(2,1)}), bf16[16,40,256]{2,1,0:T(8,128)(2,1)S(1)}, u32[]{:S(2)}, u32[]{:S(2)}) async-start(bf16[16,40,256]{2,1,0:T(8,128)(2,1)} %broadcast_in_dim.8), calls=%async_computation | async-start | bytes 655360 | tf_op jit(solution)/shard_map/all_to_all | solution.py:35
  17.4 2.5 %broadcast_select_fusion = (bf16[64,5120]{1,0:T(8,128)(2,1)}, bf16[64,5120]{1,0:T(8,128)(2,1)}) fusion(pred[]{:T(512)S(6)} %eq.22, bf16[256,5120]{1,0:T(8,128)(2,1)} %param.8), kind=kLoop, calls=%fused_computation.36 | loop fusion | flops 655360 | bytes 2621441 | tf_op jit(solution)/shard_map/jit(_where)/select_n | solution.py:141
  19.8 3.2 %collective-permute-start = (bf16[64,5120]{1,0:T(8,128)(2,1)}, bf16[64,5120]{1,0:T(8,128)(2,1)}, u32[]{:S(2)}, u32[]{:S(2)}) collective-permute-start(bf16[64,5120]{1,0:T(8,128)(2,1)} %get-tuple-element.20), channel_id=1, source_target_pairs={{0,4},{4,0},{8,12},{12,8},{16,20},{20,16},{24,28},{28,24},{32,36},... | collective-permute-start | bytes 1966088 | tf_op jit(solution)/shard_map/ppermute | solution.py:140
  23.0 0.7 collective-permute-start.1
  23.8 0.0 copy-done.9
  23.8 0.0 copy-done.10
  23.8 0.1 copy.25
  23.9 0.1 convert_reduce_fusion.1
  24.0 0.4 convert_reduce_fusion
  24.5 13.7 %all-to-all-done = bf16[16,40,256]{2,1,0:T(8,128)(2,1)S(1)} async-done(((bf16[16,40,256]{2,1,0:T(8,128)(2,1)}), bf16[16,40,256]{2,1,0:T(8,128)(2,1)S(1)}, u32[]{:S(2)}, u32[]{:S(2)}) %all-to-all-start) | async-done | bytes 327712 | tf_op jit(solution)/shard_map/all_to_all | solution.py:35
  38.1 1.7 %broadcast_in_dim.9 = bf16[8,16,40,256]{3,2,1,0:T(8,128)(2,1)} broadcast(bf16[16,40,256]{2,1,0:T(8,128)(2,1)S(1)} %all-to-all-done), dimensions={1,2,3} | broadcast | bytes 2949120 | tf_op jit(solution)/shard_map/broadcast_in_dim | solution.py:30
  39.8 0.0 copy-start.4
  39.8 6.5 %all-to-all-start.1 = ((bf16[8,16,40,256]{3,2,1,0:T(8,128)(2,1)}), bf16[8,16,40,256]{3,2,1,0:T(8,128)(2,1)}, u32[]{:S(2)}, u32[]{:S(2)}) async-start(bf16[8,16,40,256]{3,2,1,0:T(8,128)(2,1)} %broadcast_in_dim.9), calls=%async_computation.1 | async-start | bytes 5242880 | tf_op jit(solution)/shard_map/all_to_all | solution.py:37
  46.3 0.0 copy-start.8
  46.3 4.7 %collective-permute-done = bf16[64,5120]{1,0:T(8,128)(2,1)} collective-permute-done((bf16[64,5120]{1,0:T(8,128)(2,1)}, bf16[64,5120]{1,0:T(8,128)(2,1)}, u32[]{:S(2)}, u32[]{:S(2)}) %collective-permute-start) | collective-permute-done | bytes 655392 | tf_op jit(solution)/shard_map/ppermute | solution.py:140
  51.1 1.3 %fusion.9 = f32[64]{0:T(128)S(1)} fusion(bf16[64,5120]{1,0:T(8,128)(2,1)} %collective-permute-done), kind=kLoop, calls=%fused_computation.17 | loop fusion | flops 982976 | bytes 655616 | tf_op jit(solution)/shard_map/reduce_sum | solution.py:46
  52.4 0.0 copy-done.4
  52.4 0.6 fusion.2
  53.0 0.0 collective-permute-done.1
  53.0 0.0 copy-done.8
  53.1 0.0 copy-start.5
  53.1 1.0 fusion.5
  54.1 0.0 copy-done.5
  54.1 0.2 fusion.12
  54.3 0.0 copy-start.6
  54.3 1.7 %convolution_add_fusion.1 = f32[128,5120]{1,0:T(8,128)S(1)} fusion(f32[128,5120]{1,0:T(8,128)S(1)} %fusion.5, bf16[64,5120]{1,0:T(8,128)(2,1)} %collective-permute-done, f32[5120]{0:T(1024)S(1)} %copy-done.8, f32[64]{0:T(128)S(1)} %add_rsqrt_fusion.2, bf16[128,64]{0,1:T(8,128)(2,1)S(1)} %get-tuple-element.18), kind=kOutput, calls=%fused_computation.4 | convolution fusion | flops 85852160 | bytes 5935360 | tf_op jit(solution)/shard_map/dot_general | solution.py:159
  56.1 0.0 copy-start.1
  56.1 0.0 copy-done.6
  56.1 0.6 fusion.1
  56.7 1.9 %collective-permute-start.2 = (bf16[128,5120]{1,0:T(8,128)(2,1)S(1)}, bf16[128,5120]{1,0:T(8,128)(2,1)}, u32[]{:S(2)}, u32[]{:S(2)}) collective-permute-start(bf16[128,5120]{1,0:T(8,128)(2,1)S(1)} %fusion.1), channel_id=1, source_target_pairs={{0,1},{1,0},{2,3},{3,2},{4,5},{5,4},{6,7},{7,6},{8,9},{9,8},{10,11... | collective-permute-start | bytes 3932168 | tf_op jit(solution)/shard_map/ppermute | solution.py:171
  59.3 0.0 copy-done.1
  59.3 0.3 multiply_reduce_fusion
  59.6 17.8 %all-to-all-done.1 = bf16[8,16,40,256]{3,2,1,0:T(8,128)(2,1)} async-done(((bf16[8,16,40,256]{3,2,1,0:T(8,128)(2,1)}), bf16[8,16,40,256]{3,2,1,0:T(8,128)(2,1)}, u32[]{:S(2)}, u32[]{:S(2)}) %all-to-all-start.1) | async-done | bytes 2621472 | tf_op jit(solution)/shard_map/all_to_all | solution.py:37
  77.3 2.0 %copy.26 = bf16[16,8,40,256]{3,2,1,0:T(8,128)(2,1)S(1)} copy(bf16[16,8,40,256]{3,2,0,1:T(8,128)(2,1)} %bitcast.3) | data formatting | bytes 5242880 | tf_op jit(solution)/shard_map/transpose | solution.py:40
  79.3 0.0 copy-start.3
  79.3 0.0 collective-permute-done.2
  79.3 3.7 %fusion.24 = bf16[8,128,256]{2,1,0:T(8,128)(2,1)} fusion(bf16[8,640,256]{2,1,0:T(8,128)(2,1)S(1)} %bitcast.29, bf16[16,8,8,640]{3,2,1,0:T(8,128)(2,1)} %bitcast.11), kind=kOutput, calls=%fused_computation.30 | convolution fusion | flops 335806464 | bytes 4456448 | tf_op jit(solution)/shard_map/rgk,gkm->grm/dot_general | solution.py:176
  83.0 0.0 copy-start.2
  83.0 2.0 %collective-permute-start.3 = (bf16[8,128,256]{2,1,0:T(8,128)(2,1)}, bf16[8,128,256]{2,1,0:T(8,128)(2,1)S(1)}, u32[]{:S(2)}, u32[]{:S(2)}) collective-permute-start(bf16[8,128,256]{2,1,0:T(8,128)(2,1)} %fusion.24), channel_id=1, source_target_pairs={{0,1},{1,0},{2,3},{3,2},{4,5},{5,4},{6,7},{7,6},{8,9},{9,8},{10,11... | collective-permute-start | bytes 1572872 | tf_op jit(solution)/shard_map/ppermute | solution.py:179
  85.1 0.0 copy-done.3
  85.1 0.1 copy.30.inv_ref
  85.2 2.4 %fusion.21.own_ref = bf16[8,128,256]{2,1,0:T(8,128)(2,1)S(1)} fusion(bf16[8,640,256]{2,1,0:T(8,128)(2,1)} %bitcast.30, bf16[16,8,8,640]{3,2,1,0:T(8,128)(2,1)S(1)} %bitcast.31), kind=kOutput, calls=%fused_computation.29 | convolution fusion | flops 335806464 | bytes 4456448 | tf_op jit(solution)/shard_map/rgk,gkm->grm/dot_general | solution.py:176
  87.6 0.0 collective-permute-done.3.back_ref
  87.6 0.0 copy-done.2
  87.6 1.9 %shard_map.103 = (f32[128,128]{1,0:T(8,128)}, f32[128,1]{1,0:T(8,128)S(1)}) custom-call(s32[1]{0:T(128)} %bitcast.core_ref, s32[1]{0:T(128)S(6)} %copy.46.count_ref, bf16[128,4096]{1,0:T(8,128)(2,1)S(1)} %copy-done.1, f32[128,1]{1,0:T(8,128)S(1)} %copy.30.inv_ref, f32[1,4096]{1,0:T(1,128)S(1)} %bitcast.27, bf16[8,128,256]{2,1,0:T(8,128)(2,1)S(1)} %fusion.21.own_ref, ...), custom_call_target="tpu_custom_call" | custom-call | flops 8000000 | bytes 2200000 | tf_op jit(solution)/shard_map/pallas_call | solution.py:196
  89.4 16.8 %all-to-all-start.2 = ((f32[128,1,128]{2,1,0:T(1,128)}), f32[128,1,128]{2,1,0:T(1,128)S(1)}, u32[]{:S(2)}, u32[]{:S(2)}) async-start(f32[128,1,128]{2,1,0:T(1,128)} %bitcast.6), calls=%async_computation.2 | async-start | bytes 131072 | tf_op jit(solution)/shard_map/all_to_all | solution.py:216
  106.2 2.2 %shard_map.104 = bf16[128,4096]{1,0:T(8,128)(2,1)} custom-call(s32[1]{0:T(128)} %bitcast.core_ref, s32[1]{0:T(128)S(6)} %copy.46.count_ref, bf16[128,4096]{1,0:T(8,128)(2,1)S(1)} %copy-done.1, f32[128,1]{1,0:T(8,128)S(1)} %copy.30.inv_ref, f32[1,4096]{1,0:T(1,128)S(1)} %bitcast.28, bf16[8,128,256]{2,1,0:T(8,128)(2,1)S(1)} %fusion.21.own_ref, ...), custom_call_target="tpu_custom_call" | custom-call | flops 8000000 | bytes 3200000 | tf_op jit(solution)/shard_map/pallas_call | solution.py:207
  108.4 13.0 %all-to-all-done.2 = f32[128,1,128]{2,1,0:T(1,128)S(1)} async-done(((f32[128,1,128]{2,1,0:T(1,128)}), f32[128,1,128]{2,1,0:T(1,128)S(1)}, u32[]{:S(2)}, u32[]{:S(2)}) %all-to-all-start.2) | async-done | bytes 65568 | tf_op jit(solution)/shard_map/all_to_all | solution.py:216
  121.4 0.0 copy-start.7
  121.4 0.6 copy-done.7
  122.0 1.6 %shard_map.105 = (f32[32]{0:T(128)}, f32[1]{0:T(128)}) custom-call(f32[128,128]{1,0:T(8,128)} %bitcast.32), custom_call_target="tpu_custom_call" | custom-call | tf_op jit(solution)/shard_map/pallas_call | solution.py:217
  (9 shorter events, 0.1 us)
Async XLA Ops:
  0.6 0.8 copy-start
  0.6 23.1 %copy-start.9 = (s32[128,8]{0,1:T(8,128)S(1)}, s32[128,8]{0,1:T(8,128)}, u32[]{:S(2)}) copy-start(s32[128,8]{0,1:T(8,128)} %param.14) | copy-start | bytes 12292
  0.7 23.1 %copy-start.10 = (s32[128]{0:T(128)S(1)}, s32[128]{0:T(128)}, u32[]{:S(2)}) copy-start(s32[128]{0:T(128)} %param.15) | copy-start | bytes 1540
  2.2 36.0 %all-to-all-start = ((bf16[16,40,256]{2,1,0:T(8,128)(2,1)}), bf16[16,40,256]{2,1,0:T(8,128)(2,1)S(1)}, u32[]{:S(2)}, u32[]{:S(2)}) async-start(bf16[16,40,256]{2,1,0:T(8,128)(2,1)} %broadcast_in_dim.8), calls=%async_computation | async-start | bytes 655360 | tf_op jit(solution)/shard_map/all_to_all | solution.py:35
  19.8 31.2 %collective-permute-start = (bf16[64,5120]{1,0:T(8,128)(2,1)}, bf16[64,5120]{1,0:T(8,128)(2,1)}, u32[]{:S(2)}, u32[]{:S(2)}) collective-permute-start(bf16[64,5120]{1,0:T(8,128)(2,1)} %get-tuple-element.20), channel_id=1, source_target_pairs={{0,4},{4,0},{8,12},{12,8},{16,20},{20,16},{24,28},{28,24},{32,36},... | collective-permute-start | bytes 1966088 | tf_op jit(solution)/shard_map/ppermute | solution.py:140
  23.0 30.0 %collective-permute-start.1 = (bf16[64,5120]{1,0:T(8,128)(2,1)}, bf16[64,5120]{1,0:T(8,128)(2,1)S(1)}, u32[]{:S(2)}, u32[]{:S(2)}) collective-permute-start(bf16[64,5120]{1,0:T(8,128)(2,1)} %get-tuple-element.19), channel_id=1, source_target_pairs={{4,8},{8,4},{12,16},{16,12},{20,24},{24,20},{28,32},{32,28},{36,40... | collective-permute-start | bytes 1966088 | tf_op jit(solution)/shard_map/ppermute | solution.py:141
  39.8 12.6 %copy-start.4 = (bf16[256,5120]{1,0:T(8,128)(2,1)S(1)}, bf16[256,5120]{1,0:T(8,128)(2,1)}, u32[]{:S(2)}) copy-start(bf16[256,5120]{1,0:T(8,128)(2,1)} %param.8) | copy-start | bytes 7864324
  39.8 37.5 %all-to-all-start.1 = ((bf16[8,16,40,256]{3,2,1,0:T(8,128)(2,1)}), bf16[8,16,40,256]{3,2,1,0:T(8,128)(2,1)}, u32[]{:S(2)}, u32[]{:S(2)}) async-start(bf16[8,16,40,256]{3,2,1,0:T(8,128)(2,1)} %broadcast_in_dim.9), calls=%async_computation.1 | async-start | bytes 5242880 | tf_op jit(solution)/shard_map/all_to_all | solution.py:37
  46.3 6.7 %copy-start.8 = (f32[5120]{0:T(1024)S(1)}, f32[5120]{0:T(1024)}, u32[]{:S(2)}) copy-start(f32[5120]{0:T(1024)} %param.9) | copy-start | bytes 61444
  53.1 1.0 copy-start.5
  54.3 1.8 %copy-start.6 = (bf16[64,5120]{1,0:T(8,128)(2,1)S(1)}, bf16[64,5120]{1,0:T(8,128)(2,1)}, u32[]{:S(2)}) copy-start(bf16[64,5120]{1,0:T(8,128)(2,1)} %copy-done.5) | copy-start | bytes 1966084
  56.1 3.2 %copy-start.1 = (bf16[128,4096]{1,0:T(8,128)(2,1)S(1)}, bf16[128,4096]{1,0:T(8,128)(2,1)}, u32[]{:S(2)}) copy-start(bf16[128,4096]{1,0:T(8,128)(2,1)} %student_ref.3) | copy-start | bytes 3145732
  56.7 22.6 %collective-permute-start.2 = (bf16[128,5120]{1,0:T(8,128)(2,1)S(1)}, bf16[128,5120]{1,0:T(8,128)(2,1)}, u32[]{:S(2)}, u32[]{:S(2)}) collective-permute-start(bf16[128,5120]{1,0:T(8,128)(2,1)S(1)} %fusion.1), channel_id=1, source_target_pairs={{0,1},{1,0},{2,3},{3,2},{4,5},{5,4},{6,7},{7,6},{8,9},{9,8},{10,11... | collective-permute-start | bytes 3932168 | tf_op jit(solution)/shard_map/ppermute | solution.py:171
  79.3 5.7 %copy-start.3 = (bf16[16,8,40,256]{3,2,1,0:T(8,128)(2,1)}, bf16[16,8,40,256]{3,2,1,0:T(8,128)(2,1)S(1)}, u32[]{:S(2)}) copy-start(bf16[16,8,40,256]{3,2,1,0:T(8,128)(2,1)S(1)} %copy.26) | copy-start | bytes 7864324
  83.0 4.6 %copy-start.2 = (f32[4096]{0:T(1024)S(1)}, f32[4096]{0:T(1024)}, u32[]{:S(2)}) copy-start(f32[4096]{0:T(1024)} %param.12) | copy-start | bytes 49156
  83.0 4.6 %collective-permute-start.3 = (bf16[8,128,256]{2,1,0:T(8,128)(2,1)}, bf16[8,128,256]{2,1,0:T(8,128)(2,1)S(1)}, u32[]{:S(2)}, u32[]{:S(2)}) collective-permute-start(bf16[8,128,256]{2,1,0:T(8,128)(2,1)} %fusion.24), channel_id=1, source_target_pairs={{0,1},{1,0},{2,3},{3,2},{4,5},{5,4},{6,7},{7,6},{8,9},{9,8},{10,11... | collective-permute-start | bytes 1572872 | tf_op jit(solution)/shard_map/ppermute | solution.py:179
  89.4 31.9 %all-to-all-start.2 = ((f32[128,1,128]{2,1,0:T(1,128)}), f32[128,1,128]{2,1,0:T(1,128)S(1)}, u32[]{:S(2)}, u32[]{:S(2)}) async-start(f32[128,1,128]{2,1,0:T(1,128)} %bitcast.6), calls=%async_computation.2 | async-start | bytes 131072 | tf_op jit(solution)/shard_map/all_to_all | solution.py:216
  121.4 0.6 copy-start.7

commit v4 on v3

--- a/solution.py
+++ b/solution.py
@@ -137,8 +137,10 @@
     across = [(i, i + 1 if i % 2 else i - 1) for i in range(1, DEVICES - 1)]
     head = teacher_hidden[:HALO]
     tail = teacher_hidden[row_count - HALO :]
-    inner = lax.ppermute(jnp.where(lo == 0, tail, head), CTX, within)
-    outer = lax.ppermute(jnp.where(lo == 0, head, tail), CTX, across)
+    far = jnp.where(lo == 0, head, tail)
+    outer = lax.ppermute(far, CTX, across)
+    near = lax.optimization_barrier((jnp.where(lo == 0, tail, head), far))[0]
+    inner = lax.ppermute(near, CTX, within)
 
     weights, line = gather_columns(group_proj)
     teacher_hidden = lax.optimization_barrier((teacher_hidden, line))[0]

time: 124 us -> 124 us (level)
  starting transfers between devices: 46.3 us -> 49.9 us
  waiting for transfers between devices: 49.2 us -> 45.6 us
    ppermute x2, starting transfers between devices: 3.88 us -> 6.76 us  [the longest x1 6.07 us: per_device(): inner = lax.ppermute(near, CTX, within)]
    all_to_all x1, waiting for transfers between devices: 13.7 us -> 10.8 us  [gather_columns(): line = lax.all_to_all(shared(mine, NZ), 'z', 0, 0)]
    all_to_all x1, waiting for transfers between devices: 17.8 us -> 16.4 us  [gather_columns(): lax.all_to_all(shared(line, NX * NY), ('x', 'ylo', 'yhi'), 0, 0, axis_ind...]
where the time goes in v4:
time: 124 us
  starting transfers between devices  49.9 us (40%)
  waiting for transfers between devices  45.6 us (37%)
  matrix products  9.35 us (8%)
  local copies, waits for them, and re-layouts  6.03 us (5%)
  Pallas kernels  5.65 us (5%)
  other arithmetic  5.49 us (4%)
  between operations  1.61 us (1%)
    all_to_all x1, starting transfers between devices, per_device(): terms = lax.all_to_all(terms, CTX, 0, 0, tiled=True)  17.2 us
    all_to_all x1, waiting for transfers between devices, gather_columns(): lax.all_to_all(shared(line, NX * NY), ('x', 'ylo', 'yhi'), 0, 0, axis_ind...  16.4 us
    all_to_all x1, starting transfers between devices, gather_columns(): line = lax.all_to_all(shared(mine, NZ), 'z', 0, 0)  15.2 us
    all_to_all x1, waiting for transfers between devices, per_device(): terms = lax.all_to_all(terms, CTX, 0, 0, tiled=True)  13 us
    all_to_all x1, waiting for transfers between devices, gather_columns(): line = lax.all_to_all(shared(mine, NZ), 'z', 0, 0)  10.8 us
    all_to_all x1, starting transfers between devices, gather_columns(): lax.all_to_all(shared(line, NX * NY), ('x', 'ylo', 'yhi'), 0, 0, axis_ind...  6.77 us
    ppermute x1, starting transfers between devices, per_device(): inner = lax.ppermute(near, CTX, within)  6.07 us
    dot_general x2, matrix products, projected(): jnp.einsum('rgk,gkm->grm', rows, weights, preferred_element_type=jnp.floa...  6.02 us
  transfers between devices with their start and end apart: 7, of which 4 were waited for; matrix products, arithmetic and copies ran while one was open for 12% of the time, Pallas kernels for 2%

profile of v4, /device:TPU:16, one launch (start us, length us, event | category | flops | bytes accessed | tf_op | source)
XLA Modules:
  0.0 123.6 jit_solution(8482790925620615765)
XLA Ops:
  0.6 0.0 copy-start
  0.6 0.0 copy-start.9
  0.7 0.0 copy-start.10
  0.7 0.7 copy-done
  1.4 0.7 broadcast_in_dim.8
  2.2 15.2 %all-to-all-start = ((bf16[16,40,256]{2,1,0:T(8,128)(2,1)}), bf16[16,40,256]{2,1,0:T(8,128)(2,1)S(1)}, u32[]{:S(2)}, u32[]{:S(2)}) async-start(bf16[16,40,256]{2,1,0:T(8,128)(2,1)} %broadcast_in_dim.8), calls=%async_computation | async-start | bytes 655360 | tf_op jit(solution)/shard_map/all_to_all | solution.py:35
  17.4 2.5 %broadcast_select_fusion = (bf16[64,5120]{1,0:T(8,128)(2,1)}, bf16[64,5120]{1,0:T(8,128)(2,1)}) fusion(pred[]{:T(512)S(6)} %eq.22, bf16[256,5120]{1,0:T(8,128)(2,1)} %param.8), kind=kLoop, calls=%fused_computation.36 | loop fusion | flops 655360 | bytes 2621441 | tf_op jit(solution)/shard_map/jit(_where)/select_n | solution.py:140
  19.8 0.7 collective-permute-start.1
  20.5 6.1 %collective-permute-start = (bf16[64,5120]{1,0:T(8,128)(2,1)}, bf16[64,5120]{1,0:T(8,128)(2,1)}, u32[]{:S(2)}, u32[]{:S(2)}) collective-permute-start(bf16[64,5120]{1,0:T(8,128)(2,1)} %get-tuple-element.12), channel_id=1, source_target_pairs={{0,4},{4,0},{8,12},{12,8},{16,20},{20,16},{24,28},{28,24},{32,36},... | collective-permute-start | bytes 1966088 | tf_op jit(solution)/shard_map/ppermute | solution.py:143
  26.6 0.0 copy-done.9
  26.7 0.0 copy-done.10
  26.7 0.1 copy.25
  26.8 0.1 convert_reduce_fusion.1
  26.9 0.4 convert_reduce_fusion
  27.3 10.8 %all-to-all-done = bf16[16,40,256]{2,1,0:T(8,128)(2,1)S(1)} async-done(((bf16[16,40,256]{2,1,0:T(8,128)(2,1)}), bf16[16,40,256]{2,1,0:T(8,128)(2,1)S(1)}, u32[]{:S(2)}, u32[]{:S(2)}) %all-to-all-start) | async-done | bytes 327712 | tf_op jit(solution)/shard_map/all_to_all | solution.py:35
  38.1 1.7 %broadcast_in_dim.9 = bf16[8,16,40,256]{3,2,1,0:T(8,128)(2,1)} broadcast(bf16[16,40,256]{2,1,0:T(8,128)(2,1)S(1)} %all-to-all-done), dimensions={1,2,3} | broadcast | bytes 2949120 | tf_op jit(solution)/shard_map/broadcast_in_dim | solution.py:30
  39.8 0.0 copy-start.4
  39.8 6.8 %all-to-all-start.1 = ((bf16[8,16,40,256]{3,2,1,0:T(8,128)(2,1)}), bf16[8,16,40,256]{3,2,1,0:T(8,128)(2,1)}, u32[]{:S(2)}, u32[]{:S(2)}) async-start(bf16[8,16,40,256]{3,2,1,0:T(8,128)(2,1)} %broadcast_in_dim.9), calls=%async_computation.1 | async-start | bytes 5242880 | tf_op jit(solution)/shard_map/all_to_all | solution.py:37
  46.6 0.0 copy-start.8
  46.6 5.4 %collective-permute-done = bf16[64,5120]{1,0:T(8,128)(2,1)} collective-permute-done((bf16[64,5120]{1,0:T(8,128)(2,1)}, bf16[64,5120]{1,0:T(8,128)(2,1)}, u32[]{:S(2)}, u32[]{:S(2)}) %collective-permute-start) | collective-permute-done | bytes 655392 | tf_op jit(solution)/shard_map/ppermute | solution.py:143
  52.0 1.3 %fusion.9 = f32[64]{0:T(128)S(1)} fusion(bf16[64,5120]{1,0:T(8,128)(2,1)} %collective-permute-done), kind=kLoop, calls=%fused_computation.17 | loop fusion | flops 982976 | bytes 655616 | tf_op jit(solution)/shard_map/reduce_sum | solution.py:46
  53.3 0.0 copy-done.4
  53.3 0.6 fusion.2
  53.9 0.0 collective-permute-done.1
  53.9 0.0 copy-done.8
  54.0 0.0 copy-start.5
  54.0 1.0 fusion.5
  55.0 0.0 copy-done.5
  55.0 0.2 fusion.12
  55.2 0.0 copy-start.6
  55.2 1.7 %convolution_add_fusion.1 = f32[128,5120]{1,0:T(8,128)S(1)} fusion(f32[128,5120]{1,0:T(8,128)S(1)} %fusion.5, bf16[64,5120]{1,0:T(8,128)(2,1)} %collective-permute-done, f32[5120]{0:T(1024)S(1)} %copy-done.8, f32[64]{0:T(128)S(1)} %add_rsqrt_fusion.2, bf16[128,64]{0,1:T(8,128)(2,1)S(1)} %get-tuple-element.20), kind=kOutput, calls=%fused_computation.4 | convolution fusion | flops 85852160 | bytes 5935360 | tf_op jit(solution)/shard_map/dot_general | solution.py:161
  57.0 0.0 copy-start.1
  57.0 0.0 copy-done.6
  57.0 0.6 fusion.1
  57.6 1.9 %collective-permute-start.2 = (bf16[128,5120]{1,0:T(8,128)(2,1)S(1)}, bf16[128,5120]{1,0:T(8,128)(2,1)}, u32[]{:S(2)}, u32[]{:S(2)}) collective-permute-start(bf16[128,5120]{1,0:T(8,128)(2,1)S(1)} %fusion.1), channel_id=1, source_target_pairs={{0,1},{1,0},{2,3},{3,2},{4,5},{5,4},{6,7},{7,6},{8,9},{9,8},{10,11... | collective-permute-start | bytes 3932168 | tf_op jit(solution)/shard_map/ppermute | solution.py:173
  60.2 0.0 copy-done.1
  60.2 0.3 multiply_reduce_fusion
  60.5 16.4 %all-to-all-done.1 = bf16[8,16,40,256]{3,2,1,0:T(8,128)(2,1)} async-done(((bf16[8,16,40,256]{3,2,1,0:T(8,128)(2,1)}), bf16[8,16,40,256]{3,2,1,0:T(8,128)(2,1)}, u32[]{:S(2)}, u32[]{:S(2)}) %all-to-all-start.1) | async-done | bytes 2621472 | tf_op jit(solution)/shard_map/all_to_all | solution.py:37
  76.8 2.0 %copy.26 = bf16[16,8,40,256]{3,2,1,0:T(8,128)(2,1)S(1)} copy(bf16[16,8,40,256]{3,2,0,1:T(8,128)(2,1)} %bitcast.3) | data formatting | bytes 5242880 | tf_op jit(solution)/shard_map/transpose | solution.py:40
  78.9 0.0 copy-start.3
  78.9 0.0 collective-permute-done.2
  78.9 3.7 %fusion.24 = bf16[8,128,256]{2,1,0:T(8,128)(2,1)} fusion(bf16[8,640,256]{2,1,0:T(8,128)(2,1)S(1)} %bitcast.29, bf16[16,8,8,640]{3,2,1,0:T(8,128)(2,1)} %bitcast.11), kind=kOutput, calls=%fused_computation.30 | convolution fusion | flops 335806464 | bytes 4456448 | tf_op jit(solution)/shard_map/rgk,gkm->grm/dot_general | solution.py:178
  82.5 0.0 copy-start.2
  82.5 2.0 %collective-permute-start.3 = (bf16[8,128,256]{2,1,0:T(8,128)(2,1)}, bf16[8,128,256]{2,1,0:T(8,128)(2,1)S(1)}, u32[]{:S(2)}, u32[]{:S(2)}) collective-permute-start(bf16[8,128,256]{2,1,0:T(8,128)(2,1)} %fusion.24), channel_id=1, source_target_pairs={{0,1},{1,0},{2,3},{3,2},{4,5},{5,4},{6,7},{7,6},{8,9},{9,8},{10,11... | collective-permute-start | bytes 1572872 | tf_op jit(solution)/shard_map/ppermute | solution.py:181
  84.6 0.0 copy-done.3
  84.6 0.1 copy.30.inv_ref
  84.7 2.4 %fusion.21.own_ref = bf16[8,128,256]{2,1,0:T(8,128)(2,1)S(1)} fusion(bf16[8,640,256]{2,1,0:T(8,128)(2,1)} %bitcast.30, bf16[16,8,8,640]{3,2,1,0:T(8,128)(2,1)S(1)} %bitcast.31), kind=kOutput, calls=%fused_computation.29 | convolution fusion | flops 335806464 | bytes 4456448 | tf_op jit(solution)/shard_map/rgk,gkm->grm/dot_general | solution.py:178
  87.1 0.0 collective-permute-done.3.back_ref
  87.1 0.0 copy-done.2
  87.1 1.9 %shard_map.103 = (f32[128,128]{1,0:T(8,128)}, f32[128,1]{1,0:T(8,128)S(1)}) custom-call(s32[1]{0:T(128)} %bitcast.core_ref, s32[1]{0:T(128)S(6)} %copy.46.count_ref, bf16[128,4096]{1,0:T(8,128)(2,1)S(1)} %copy-done.1, f32[128,1]{1,0:T(8,128)S(1)} %copy.30.inv_ref, f32[1,4096]{1,0:T(1,128)S(1)} %bitcast.27, bf16[8,128,256]{2,1,0:T(8,128)(2,1)S(1)} %fusion.21.own_ref, ...), custom_call_target="tpu_custom_call" | custom-call | flops 8000000 | bytes 2200000 | tf_op jit(solution)/shard_map/pallas_call | solution.py:198
  89.0 17.2 %all-to-all-start.2 = ((f32[128,1,128]{2,1,0:T(1,128)}), f32[128,1,128]{2,1,0:T(1,128)S(1)}, u32[]{:S(2)}, u32[]{:S(2)}) async-start(f32[128,1,128]{2,1,0:T(1,128)} %bitcast.6), calls=%async_computation.2 | async-start | bytes 131072 | tf_op jit(solution)/shard_map/all_to_all | solution.py:218
  106.2 2.2 %shard_map.104 = bf16[128,4096]{1,0:T(8,128)(2,1)} custom-call(s32[1]{0:T(128)} %bitcast.core_ref, s32[1]{0:T(128)S(6)} %copy.46.count_ref, bf16[128,4096]{1,0:T(8,128)(2,1)S(1)} %copy-done.1, f32[128,1]{1,0:T(8,128)S(1)} %copy.30.inv_ref, f32[1,4096]{1,0:T(1,128)S(1)} %bitcast.28, bf16[8,128,256]{2,1,0:T(8,128)(2,1)S(1)} %fusion.21.own_ref, ...), custom_call_target="tpu_custom_call" | custom-call | flops 8000000 | bytes 3200000 | tf_op jit(solution)/shard_map/pallas_call | solution.py:209
  108.4 13.0 %all-to-all-done.2 = f32[128,1,128]{2,1,0:T(1,128)S(1)} async-done(((f32[128,1,128]{2,1,0:T(1,128)}), f32[128,1,128]{2,1,0:T(1,128)S(1)}, u32[]{:S(2)}, u32[]{:S(2)}) %all-to-all-start.2) | async-done | bytes 65568 | tf_op jit(solution)/shard_map/all_to_all | solution.py:218
  121.4 0.0 copy-start.7
  121.4 0.6 copy-done.7
  122.0 1.6 %shard_map.105 = (f32[32]{0:T(128)}, f32[1]{0:T(128)}) custom-call(f32[128,128]{1,0:T(8,128)} %bitcast.32), custom_call_target="tpu_custom_call" | custom-call | tf_op jit(solution)/shard_map/pallas_call | solution.py:219
  (9 shorter events, 0.1 us)
Async XLA Ops:
  0.6 0.8 copy-start
  0.6 26.0 %copy-start.9 = (s32[128,8]{0,1:T(8,128)S(1)}, s32[128,8]{0,1:T(8,128)}, u32[]{:S(2)}) copy-start(s32[128,8]{0,1:T(8,128)} %param.14) | copy-start | bytes 12292
  0.7 26.0 %copy-start.10 = (s32[128]{0:T(128)S(1)}, s32[128]{0:T(128)}, u32[]{:S(2)}) copy-start(s32[128]{0:T(128)} %param.15) | copy-start | bytes 1540
  2.2 36.0 %all-to-all-start = ((bf16[16,40,256]{2,1,0:T(8,128)(2,1)}), bf16[16,40,256]{2,1,0:T(8,128)(2,1)S(1)}, u32[]{:S(2)}, u32[]{:S(2)}) async-start(bf16[16,40,256]{2,1,0:T(8,128)(2,1)} %broadcast_in_dim.8), calls=%async_computation | async-start | bytes 655360 | tf_op jit(solution)/shard_map/all_to_all | solution.py:35
  19.8 34.1 %collective-permute-start.1 = (bf16[64,5120]{1,0:T(8,128)(2,1)}, bf16[64,5120]{1,0:T(8,128)(2,1)S(1)}, u32[]{:S(2)}, u32[]{:S(2)}) collective-permute-start(bf16[64,5120]{1,0:T(8,128)(2,1)} %get-tuple-element.21), channel_id=1, source_target_pairs={{4,8},{8,4},{12,16},{16,12},{20,24},{24,20},{28,32},{32,28},{36,40... | collective-permute-start | bytes 1966088 | tf_op jit(solution)/shard_map/ppermute | solution.py:141
  20.5 31.4 %collective-permute-start = (bf16[64,5120]{1,0:T(8,128)(2,1)}, bf16[64,5120]{1,0:T(8,128)(2,1)}, u32[]{:S(2)}, u32[]{:S(2)}) collective-permute-start(bf16[64,5120]{1,0:T(8,128)(2,1)} %get-tuple-element.12), channel_id=1, source_target_pairs={{0,4},{4,0},{8,12},{12,8},{16,20},{20,16},{24,28},{28,24},{32,36},... | collective-permute-start | bytes 1966088 | tf_op jit(solution)/shard_map/ppermute | solution.py:143
  39.8 13.5 %copy-start.4 = (bf16[256,5120]{1,0:T(8,128)(2,1)S(1)}, bf16[256,5120]{1,0:T(8,128)(2,1)}, u32[]{:S(2)}) copy-start(bf16[256,5120]{1,0:T(8,128)(2,1)} %param.8) | copy-start | bytes 7864324
  39.8 37.0 %all-to-all-start.1 = ((bf16[8,16,40,256]{3,2,1,0:T(8,128)(2,1)}), bf16[8,16,40,256]{3,2,1,0:T(8,128)(2,1)}, u32[]{:S(2)}, u32[]{:S(2)}) async-start(bf16[8,16,40,256]{3,2,1,0:T(8,128)(2,1)} %broadcast_in_dim.9), calls=%async_computation.1 | async-start | bytes 5242880 | tf_op jit(solution)/shard_map/all_to_all | solution.py:37
  46.6 7.4 %copy-start.8 = (f32[5120]{0:T(1024)S(1)}, f32[5120]{0:T(1024)}, u32[]{:S(2)}) copy-start(f32[5120]{0:T(1024)} %param.9) | copy-start | bytes 61444
  54.0 1.0 copy-start.5
  55.2 1.8 %copy-start.6 = (bf16[64,5120]{1,0:T(8,128)(2,1)S(1)}, bf16[64,5120]{1,0:T(8,128)(2,1)}, u32[]{:S(2)}) copy-start(bf16[64,5120]{1,0:T(8,128)(2,1)} %copy-done.5) | copy-start | bytes 1966084
  57.0 3.2 %copy-start.1 = (bf16[128,4096]{1,0:T(8,128)(2,1)S(1)}, bf16[128,4096]{1,0:T(8,128)(2,1)}, u32[]{:S(2)}) copy-start(bf16[128,4096]{1,0:T(8,128)(2,1)} %student_ref.3) | copy-start | bytes 3145732
  57.6 21.3 %collective-permute-start.2 = (bf16[128,5120]{1,0:T(8,128)(2,1)S(1)}, bf16[128,5120]{1,0:T(8,128)(2,1)}, u32[]{:S(2)}, u32[]{:S(2)}) collective-permute-start(bf16[128,5120]{1,0:T(8,128)(2,1)S(1)} %fusion.1), channel_id=1, source_target_pairs={{0,1},{1,0},{2,3},{3,2},{4,5},{5,4},{6,7},{7,6},{8,9},{9,8},{10,11... | collective-permute-start | bytes 3932168 | tf_op jit(solution)/shard_map/ppermute | solution.py:173
  78.9 5.7 %copy-start.3 = (bf16[16,8,40,256]{3,2,1,0:T(8,128)(2,1)}, bf16[16,8,40,256]{3,2,1,0:T(8,128)(2,1)S(1)}, u32[]{:S(2)}) copy-start(bf16[16,8,40,256]{3,2,1,0:T(8,128)(2,1)S(1)} %copy.26) | copy-start | bytes 7864324
  82.5 4.6 %copy-start.2 = (f32[4096]{0:T(1024)S(1)}, f32[4096]{0:T(1024)}, u32[]{:S(2)}) copy-start(f32[4096]{0:T(1024)} %param.12) | copy-start | bytes 49156
  82.5 4.6 %collective-permute-start.3 = (bf16[8,128,256]{2,1,0:T(8,128)(2,1)}, bf16[8,128,256]{2,1,0:T(8,128)(2,1)S(1)}, u32[]{:S(2)}, u32[]{:S(2)}) collective-permute-start(bf16[8,128,256]{2,1,0:T(8,128)(2,1)} %fusion.24), channel_id=1, source_target_pairs={{0,1},{1,0},{2,3},{3,2},{4,5},{5,4},{6,7},{7,6},{8,9},{9,8},{10,11... | collective-permute-start | bytes 1572872 | tf_op jit(solution)/shard_map/ppermute | solution.py:181
  89.0 32.4 %all-to-all-start.2 = ((f32[128,1,128]{2,1,0:T(1,128)}), f32[128,1,128]{2,1,0:T(1,128)S(1)}, u32[]{:S(2)}, u32[]{:S(2)}) async-start(f32[128,1,128]{2,1,0:T(1,128)} %bitcast.6), calls=%async_computation.2 | async-start | bytes 131072 | tf_op jit(solution)/shard_map/all_to_all | solution.py:218
  121.4 0.6 copy-start.7
